TPU v7x, 32 devices: a whole 2x2x4 slice. The times are simulated.
32 devices in a mesh: slab: 8 (over z, core), filt: 4 (over y, x).
Axes of the slice: x: 2, y: 2, z: 4, core: 2. Of those that a mesh axis runs over, the one named last changes fastest.
Arguments:
- features: bfloat16 [16, 512, 256], P('slab', 'filt'), may hold values from -6 to 6
- first_weight: bfloat16 [27, 512, 512], P(None, 'filt'), may hold values from -0.0546875 to 0.0546875
- second_weight: bfloat16 [27, 512, 512], P(None, 'filt'), may hold values from -0.0546875 to 0.0546875
- head_weight: bfloat16 [8, 512], P(None, 'filt'), may hold values from -0.25 to 0.25
- labels: int32 [16, 256], P('slab'), may hold values from 0 to 7
Outputs:
- first_grad: float32 [27, 512, 512], P(None, 'filt', 'slab')
- second_grad: float32 [27, 512, 512], P(None, 'filt', 'slab')
All inputs are finite; a program needn't handle non-finite values.
Results may differ from a plain program's by a relative error of at most 0.0075.
Values may be sent and summed in bfloat16 or wider, within the bound.
No kernel may reach another device: no remote copies, remote signals or barrier semaphores. Data moves between devices by JAX's collectives and lax.ppermute only.
A program may use at most 128 MiB of HBM per device.

v0:
```python
import functools

import jax
import jax.numpy as jnp
from jax import lax
from jax.experimental import pallas as pl
from jax.experimental.pallas import tpu as pltpu
from jax.sharding import PartitionSpec as P

WIDTH = 8
SHIFTS = [(b, e) for b in (-1, 0, 1) for e in (-1, 0, 1)]
LIMIT = 20 * 1024 * 1024
VMEM = pl.BlockSpec(memory_space=pltpu.VMEM)
ANY = pl.BlockSpec(memory_space=pl.ANY)


def swap(block, axis, step):
    count = lax.axis_size(axis)
    return lax.ppermute(block, axis, [(i, i ^ step) for i in range(count)])


def exchanged(block, axis):
    return [block] + [swap(block, axis, step) for step in range(1, lax.axis_size(axis))]


def halo(volume, own, due=()):
    count = lax.axis_size("slab")
    other = swap(volume, "slab", 1)
    passed = edge(other, [own, *due])
    pairs = [(i, i + 2) for i in range(0, count - 2, 2)] + [(i, i - 2) for i in range(3, count, 2)]
    return other, lax.ppermute(passed, "slab", pairs)


def chips_apart(blocks):
    return [swap(block, "slab", 2 + 2 * number) for number, block in enumerate(blocks)]


def every_chip(block):
    blocks = [block]
    for step in range(1, lax.axis_size("slab") // 2):
        low = step & -step
        blocks.append(swap(blocks[step ^ low], "slab", 2 * low))
    return blocks


def call(body, out_shape, cost, *operands, in_specs, scratch_shapes=(), passed=(), after=()):
    flops, moved = cost
    single = not isinstance(out_shape, list)
    outs = [out_shape] if single else out_shape
    first, second = len(operands), len(operands) + len(passed) + len(after)
    third = second + len(outs)

    def inner(*refs):
        body(*refs[:first], *refs[second:third], *refs[third + len(passed) :])

    given = pl.pallas_call(
        inner,
        out_shape=[*outs, *(struct(array.shape, array.dtype) for array in passed)],
        cost_estimate=pl.CostEstimate(flops=flops, bytes_accessed=moved, transcendentals=0),
        compiler_params=pltpu.CompilerParams(vmem_limit_bytes=LIMIT),
        in_specs=[*in_specs] + [ANY] * (len(passed) + len(after)),
        out_specs=[VMEM] * len(outs) + [ANY] * len(passed),
        scratch_shapes=list(scratch_shapes),
        input_output_aliases={first + i: len(outs) + i for i in range(len(passed))},
    )(*operands, *passed, *after)
    if passed:
        return [*given[: len(outs)], list(given[len(outs) :])]
    return given[0] if single else list(given)


def struct(shape, dtype):
    return jax.ShapeDtypeStruct(tuple(shape), dtype)


def here(axis):
    return lax.axis_index(axis).astype(jnp.int32)


def core():
    return lax.rem(here("slab"), 2)


def far_owners(side):
    me = here("slab")
    return [me ^ (2 * step) ^ side for step in range(lax.axis_size("slab") // 2)]


TOKEN = struct((8, 128), jnp.float32)


def stage_body(count, *refs):
    sources, targets, sems = refs[:count], refs[count : 2 * count], refs[2 * count]
    copies = [pltpu.make_async_copy(sources[i], targets[i], sems.at[i]) for i in range(count)]
    for copy in copies:
        copy.start()
    for copy in copies:
        copy.wait()


def stage(*arrays):
    count = len(arrays)
    return call(
        functools.partial(stage_body, count),
        [struct(array.shape, array.dtype) for array in arrays],
        (0, sum(4 * array.size for array in arrays)),
        *arrays,
        in_specs=[pl.BlockSpec(memory_space=pltpu.HBM)] * count,
        scratch_shapes=[pltpu.SemaphoreType.DMA((count,))],
    )


def inside(shape, axis, b, e):
    spot = lax.broadcasted_iota(jnp.int32, shape, axis)
    column = spot % WIDTH + e
    moved = spot + WIDTH * b
    return (column >= 0) & (column < WIDTH) & (moved >= 0) & (moved < shape[axis])


def shifted(values, axis, b, e):
    if b == 0 and e == 0:
        return values
    size = values.shape[axis]
    turned = pltpu.roll(values, (-(WIDTH * b + e)) % size, axis)
    return jnp.where(inside(values.shape, axis, b, e), turned, 0.0)


def fold_shifts(products):
    rows = products.shape[0] // len(SHIFTS)
    total = None
    for number, (b, e) in enumerate(SHIFTS):
        term = shifted(products[number * rows : (number + 1) * rows, :], 1, b, e)
        total = term if total is None else total + term
    return total


def dot(left, right):
    return jnp.dot(left, right, preferred_element_type=jnp.float32)


def edge_body(other_ref, out_ref):
    out_ref[0] = other_ref[(1 - core()) * (other_ref.shape[0] - 1)]


def edge(other, after):
    shape = (1, *other.shape[1:])
    return call(edge_body, struct(shape, other.dtype), (0, other.size), other, in_specs=[VMEM], after=after)


def halves(rows):
    return 2 if rows % 32 == 0 and lax.axis_size("filt") % 2 == 0 else 1


def assemble_body(count, split, *refs):
    parts, whole_ref, shares = refs[:count], refs[count], refs[count + 1 :]
    size = parts[0].shape[1]
    me, chip = here("filt"), here("slab") // 2
    for step in range(count):
        place = pl.ds(pl.multiple_of((me ^ step) * size, size), size)
        whole_ref[:, place, :] = parts[step][...]
    rows = shares[0].shape[2]
    for step, share_ref in enumerate(shares):
        for side in range(2):
            begin = (((chip ^ step) * 2 + side) * split + lax.rem(me, split)) * rows
            share_ref[side] = whole_ref[:, pl.ds(pl.multiple_of(begin, rows), rows), :]


def assemble(parts, after=()):
    planes, size, plane = parts[0].shape
    count, slabs = len(parts), lax.axis_size("slab")
    channels = size * count
    split = halves(channels // slabs)
    kind = parts[0].dtype
    outs = [struct((planes, channels, plane), kind)]
    outs += [struct((2, planes, channels // slabs // split, plane), kind)] * (slabs // 2)
    whole, *shares = call(
        functools.partial(assemble_body, count, split),
        outs,
        (0, 4 * planes * channels * plane),
        *parts,
        in_specs=[VMEM] * count,
        after=after,
    )
    return whole, shares


def crossing_body(count, *refs):
    planes = refs[0].shape[1]
    for step in range(count):
        for j in range(planes):
            refs[count][step * planes + j] = refs[step][1 - core(), j]


def collect_body(count, crossed_ref, *refs):
    owners, side = far_owners(0), core()
    planes = refs[0].shape[1]
    for step in range(count):
        for j in range(planes):
            refs[count][owners[step] * planes + j] = refs[step][side, j]
            refs[count][(owners[step] ^ 1) * planes + j] = crossed_ref[step * planes + j]


def collected(shares, after, later=()):
    count = len(shares)
    _, planes, rows, plane = shares[0].shape
    kind, size = shares[0].dtype, shares[0].size * count
    crossing = call(
        functools.partial(crossing_body, count),
        struct((count * planes, rows, plane), kind),
        (0, 2 * size),
        *shares,
        in_specs=[VMEM] * count,
        after=after,
    )
    return call(
        functools.partial(collect_body, count),
        struct((2 * count * planes, rows, plane), kind),
        (0, 4 * size),
        swap(crossing, "slab", 1), *shares,
        in_specs=[VMEM] * (1 + count),
        after=later,
    )


def both_halves(volume, split):
    return [volume] + ([swap(volume, "filt", 1)] if split == 2 else [])


def pack_body(count, *refs):
    out_ref = refs[count]
    row = 0
    for number in range(count):
        planes, plane, filters = refs[number].shape
        for j in range(planes):
            for begin in range(0, plane, filters):
                out_ref[row : row + filters, begin : begin + filters] = refs[number][j, begin : begin + filters, :]
            row += filters


def pack(blocks, after=()):
    plane = blocks[0].shape[1]
    total = sum(block.size for block in blocks)
    return call(
        functools.partial(pack_body, len(blocks)),
        struct((total // plane, plane), blocks[0].dtype),
        (0, 4 * total),
        *blocks,
        in_specs=[VMEM] * len(blocks),
        after=after,
    )


def taps(weight_ref, number):
    block = weight_ref[pl.ds(9 * number, 9)]
    return block.reshape(block.shape[0] * block.shape[1], block.shape[2])


def forward_own_body(planes, volume_ref, weight_ref, out_ref, acc_ref):
    for a in (0, 1, -1):
        weight = taps(weight_ref, a + 1)
        for j in range(planes):
            if 0 <= j + a < planes:
                product = dot(weight, volume_ref[j + a])
                acc_ref[j] = product if a == 0 else acc_ref[j] + product
    for j in range(planes):
        out_ref[j] = fold_shifts(acc_ref.at[j])


def forward_own(volume, weight):
    planes, channels, plane = volume.shape
    filters = weight.shape[1]
    return call(
        functools.partial(forward_own_body, planes),
        struct((planes, filters, plane), jnp.float32),
        (2 * 9 * filters * channels * plane * (3 * planes - 2), weight.size * 2),
        volume, weight,
        in_specs=[VMEM] * 2,
        scratch_shapes=[pltpu.VMEM((planes, 9 * filters, plane), jnp.float32)],
    )


def forward_other_body(planes, other_ref, weight_ref, own_ref, out_ref, acc_ref):
    up, last = core(), planes - 1
    place = (1 - up) * last
    acc_ref[...] = dot(taps(weight_ref, 2 * (1 - up)), other_ref[up * last])
    out_ref[...] = own_ref[...]
    out_ref[place] = out_ref[place] + fold_shifts(acc_ref)


def forward_other(other, weight, own):
    planes, filters, plane = own.shape
    return call(
        functools.partial(forward_other_body, planes),
        struct(own.shape, jnp.float32),
        (2 * weight.size // 3 * plane, weight.size * 2 // 3),
        other, weight, own,
        in_specs=[VMEM] * 3,
        scratch_shapes=[pltpu.VMEM((9 * filters, plane), jnp.float32)],
    )


def silu_and_slope(values):
    sig = 1.0 / (1.0 + jnp.exp(-values))
    return values * sig, sig * (1.0 + values * (1.0 - sig))


def forward_rest_body(planes, beyond_ref, weight_ref, own_ref, *refs):
    head_ref = refs[0] if len(refs) == 5 else None
    slope_ref, made_ref, acc_ref, total_ref = refs[-4:]
    up = core()
    place = up * (planes - 1)
    total_ref[...] = own_ref[...]
    acc_ref[...] = dot(taps(weight_ref, 2 * up), beyond_ref[0])
    total_ref[place] = total_ref[place] + fold_shifts(acc_ref)
    for j in range(planes):
        value, slope = silu_and_slope(total_ref[j])
        value = value.astype(jnp.bfloat16)
        slope_ref[j] = slope.T if head_ref is None else slope
        made_ref[j] = value if head_ref is None else dot(head_ref[...], value)


def forward_rest(beyond, weight, own, after, head=None):
    planes, filters, plane = own.shape
    channels = weight.shape[2]
    ins = [beyond, weight, own]
    slope = own.shape
    if head is None:
        slope = (planes, plane, filters)
        made = struct(own.shape, jnp.bfloat16)
    else:
        ins.append(head)
        made = struct((planes, head.shape[0], plane), jnp.float32)
    return call(
        functools.partial(forward_rest_body, planes),
        [struct(slope, jnp.float32), made],
        (2 * 9 * filters * channels * plane, weight.size * 2 // 3),
        *ins,
        in_specs=[VMEM] * len(ins),
        scratch_shapes=[
            pltpu.VMEM((9 * filters, plane), jnp.float32),
            pltpu.VMEM(own.shape, jnp.float32),
        ],
        after=after,
    )


def loss_body(count, labels_ref, head_ref, slope_ref, *refs):
    parts, grad_ref = refs[:count], refs[count]
    for j in range(grad_ref.shape[0]):
        logits = parts[0][j]
        for part in parts[1:]:
            logits = logits + part[j]
        powers = jnp.exp(logits)
        likely = powers / jnp.sum(powers, axis=0, keepdims=True)
        classes = lax.broadcasted_iota(jnp.int32, logits.shape, 0)
        onehot = (labels_ref[j : j + 1, :] == classes).astype(jnp.float32)
        logit_grad = (likely - onehot).astype(jnp.bfloat16).astype(jnp.float32)
        back = lax.dot_general(
            head_ref[...].astype(jnp.float32),
            logit_grad,
            (((0,), (0,)), ((), ())),
            preferred_element_type=jnp.float32,
        )
        grad_ref[j] = (back * slope_ref[j]).T.astype(jnp.bfloat16)


def loss_grad(parts, labels, head, slope, after):
    planes, plane = labels.shape
    return call(
        functools.partial(loss_body, len(parts)),
        struct((planes, plane, slope.shape[1]), jnp.bfloat16),
        (2 * slope.size * head.shape[0], slope.size * 6),
        labels, head, slope, *parts,
        in_specs=[VMEM] * (3 + len(parts)),
        after=after,
    )


def spread_back(grad, spread_ref):
    filters = grad.shape[1]
    turned = grad.astype(jnp.float32)
    for number, (b, e) in enumerate(SHIFTS):
        moved = shifted(turned, 0, -b, -e).astype(jnp.bfloat16)
        spread_ref[:, number * filters : (number + 1) * filters] = moved


def backward_own_body(planes, grad_ref, weight_ref, out_ref, spread_ref):
    for j in range(planes):
        spread_back(grad_ref[j], spread_ref.at[j])
    for a in (0, 1, -1):
        weight = taps(weight_ref, a + 1)
        for j in range(planes):
            if 0 <= j - a < planes:
                product = dot(spread_ref[j - a], weight)
                out_ref[j] = product if a == 0 else out_ref[j] + product


def backward_own(grad, weight):
    planes, plane, filters = grad.shape
    channels = weight.shape[2]
    return call(
        functools.partial(backward_own_body, planes),
        struct((planes, plane, channels), jnp.float32),
        (2 * 9 * filters * channels * plane * (3 * planes - 2), weight.size * 2),
        grad, weight,
        in_specs=[VMEM] * 2,
        scratch_shapes=[pltpu.VMEM((planes, plane, 9 * filters), jnp.bfloat16)],
    )


def backward_other_body(planes, other_ref, weight_ref, own_ref, out_ref, spread_ref):
    up, last = core(), planes - 1
    place = (1 - up) * last
    spread_back(other_ref[up * last], spread_ref)
    out_ref[...] = own_ref[...]
    out_ref[place] = out_ref[place] + dot(spread_ref[...], taps(weight_ref, 2 * up))


def backward_other(other, weight, own):
    planes, plane, _ = own.shape
    filters = weight.shape[1]
    return call(
        functools.partial(backward_other_body, planes),
        struct(own.shape, jnp.float32),
        (2 * weight.size // 3 * plane, weight.size * 2 // 3),
        other, weight, own,
        in_specs=[VMEM] * 3,
        scratch_shapes=[pltpu.VMEM((plane, 9 * filters), jnp.bfloat16)],
    )


def backward_rest_body(planes, count, beyond_ref, weight_ref, own_ref, *refs):
    kept_ref, sent, (spread_ref, total_ref) = refs[0], refs[1:count], refs[count:]
    size = kept_ref.shape[2]
    up, me = core(), here("filt")
    place = up * (planes - 1)
    spread_back(beyond_ref[0], spread_ref)
    product = dot(spread_ref[...], taps(weight_ref, 2 * (1 - up)))
    for block in range(count):
        columns = slice(block * size, (block + 1) * size)
        for j in range(planes):
            total_ref[block, j] = own_ref[j, :, columns]
        total_ref[block, place] = total_ref[block, place] + product[:, columns]
    kept_ref[...] = total_ref[me]
    for number in range(1, count):
        sent[number - 1][...] = total_ref[me ^ number].astype(jnp.bfloat16)


def backward_rest(beyond, weight, own, count, after):
    planes, plane, channels = own.shape
    filters = weight.shape[1]
    size = channels // count
    outs = [struct((planes, plane, size), jnp.float32)]
    outs += [struct((planes, plane, size), jnp.bfloat16)] * (count - 1)
    return call(
        functools.partial(backward_rest_body, planes, count),
        outs,
        (2 * 9 * filters * channels * plane, weight.size * 2 // 3),
        beyond, weight, own,
        in_specs=[VMEM] * 3,
        scratch_shapes=[
            pltpu.VMEM((plane, 9 * filters), jnp.bfloat16),
            pltpu.VMEM((count, planes, plane, size), jnp.float32),
        ],
        after=after,
    )


def first_grad_body(count, slope_ref, *refs):
    parts, out_ref = refs[:count], refs[count]
    for j in range(out_ref.shape[0]):
        total = parts[0][j]
        for part in parts[1:]:
            total = total + part[j].astype(jnp.float32)
        out_ref[j] = (total * slope_ref[j]).astype(jnp.bfloat16)


def first_out(parts, slope, after):
    return call(
        functools.partial(first_grad_body, len(parts)),
        struct(slope.shape, jnp.bfloat16),
        (slope.size * 4, slope.size * 14),
        slope, *parts,
        in_specs=[VMEM] * (1 + len(parts)),
        after=after,
    )


def spread_body(split, *refs):
    spread_ref, token_ref = refs[split:]
    token_ref[...] = jnp.zeros_like(token_ref)
    depth, rows, plane = refs[0].shape
    me = lax.rem(here("filt"), split)
    for d in range(depth):
        for half in range(split):
            values = refs[half][d].astype(jnp.float32)
            for number, (b, e) in enumerate(SHIFTS):
                begin = (number * split + (me ^ half)) * rows
                moved = shifted(values, 1, b, e).astype(jnp.bfloat16)
                spread_ref[pl.ds(pl.multiple_of(begin, rows), rows), d * plane : (d + 1) * plane] = moved


def spread(halved):
    split = len(halved)
    depth, rows, plane = halved[0].shape
    channels = split * rows
    return call(
        functools.partial(spread_body, split),
        [struct((9 * channels, depth * plane), jnp.bfloat16), TOKEN],
        (9 * channels * depth * plane, 10 * channels * depth * plane),
        *halved,
        in_specs=[VMEM] * split,
    )


def weight_grad_body(count, second, spread_ref, crossed_ref, *refs):
    parts, (out_ref, token_ref, grad_ref) = refs[:count], refs[count:]
    token_ref[...] = jnp.zeros_like(token_ref)
    planes, plane, filters = parts[0].shape
    channels = spread_ref.shape[0] // 9
    depth = spread_ref.shape[1] // plane
    zero = jnp.zeros((plane, filters), jnp.bfloat16)
    grad_ref[depth * plane : (depth + 1) * plane, : filters] = zero
    grad_ref[plane : 2 * plane, 2 * filters :] = zero

    def one(block, d, begin):
        rows = block.shape[0]
        for a in (-1, 0, 1):
            place = pl.ds(pl.multiple_of((d + a + 1) * plane + begin, rows), rows)
            grad_ref[place, (a + 1) * filters : (a + 2) * filters] = block

    near, far = far_owners(0), far_owners(1)
    owners = [near[0], far[0], *near[1:], *far[1:]] if second else near + far
    row = 0
    for number in range(count):
        for j in range(planes):
            one(parts[number][j], owners[number] * planes + j, 0)
    for number in range(count, len(owners)):
        for j in range(planes):
            for begin in range(0, plane, filters):
                block = crossed_ref[row : row + filters, begin : begin + filters]
                one(block, owners[number] * planes + j, begin)
            row += filters

    product = dot(spread_ref[...], grad_ref[plane : (depth + 1) * plane, :])
    for r in range(3):
        for number in range(9):
            out_ref[r * 9 + number] = product[
                number * channels : (number + 1) * channels, r * filters : (r + 1) * filters
            ]


def weight_grad(spreads, blocks, crossed, second):
    channels, columns = spreads.shape[0] // 9, spreads.shape[1]
    _, plane, filters = blocks[0].shape
    return call(
        functools.partial(weight_grad_body, len(blocks), second),
        [struct((27, channels, filters), jnp.float32), TOKEN],
        (2 * 27 * filters * channels * columns, 27 * channels * filters * 4 + spreads.size * 2),
        spreads, crossed, *blocks,
        in_specs=[VMEM] * (2 + len(blocks)),
        scratch_shapes=[pltpu.VMEM((columns + 2 * plane, 3 * filters), jnp.bfloat16)],
    )


def shards(features, first_weight, second_weight, head_weight, labels):
    count = lax.axis_size("filt")
    chips = lax.axis_size("slab") // 2
    split = halves(features.shape[1] * count // lax.axis_size("slab"))
    near, first_weight, head_weight = stage(features, first_weight, head_weight)
    all_in, share_in = assemble([near] + exchanged(features, "filt")[1:])
    own = forward_own(all_in, first_weight)
    share_in = [share_in[0]] + chips_apart(share_in[1:])
    other, beyond = halo(all_in, own, share_in[1:])
    own = forward_other(other, first_weight, own)
    slope_first, hidden = forward_rest(beyond, first_weight, own, [])

    halved_in = collected(share_in, [hidden])
    all_hidden, share_hidden = assemble(exchanged(hidden, "filt"), [halved_in])
    own = forward_own(all_hidden, second_weight)
    share_hidden = [share_hidden[0]] + chips_apart(share_hidden[1:])
    other, beyond = halo(all_hidden, own, share_hidden[1:])
    own = forward_other(other, second_weight, own)
    halved_in = both_halves(halved_in, split)
    slope_second, logits = forward_rest(beyond, second_weight, own, halved_in, head_weight)

    logits_parts = exchanged(logits, "filt")
    second_out = loss_grad(logits_parts, labels, head_weight, slope_second, [])
    halved_hidden = both_halves(collected(share_hidden, [logits], [second_out]), split)
    own = backward_own(second_out, second_weight)
    second_other, beyond = halo(second_out, own)
    second_far = every_chip(second_out)[1:]
    own = backward_other(second_other, second_weight, own)
    due = halved_hidden + second_far[chips // 2 - 1 : chips // 2]
    kept, *sent = backward_rest(beyond, second_weight, own, count, due)
    parts = [kept] + [swap(part, "filt", 1 + number) for number, part in enumerate(sent)]
    spread_in, token_in = spread(halved_in)
    spread_hidden, token_hidden = spread(halved_hidden)
    first_out_grad = first_out(parts, slope_first, [token_in, token_hidden, *second_far])

    first_blocks = [first_out_grad] + chips_apart([first_out_grad] * (chips - 1))
    crossed = swap(pack(second_far, [first_out_grad]), "slab", 1)
    second_blocks = [second_out, second_other] + second_far
    second_grad, token = weight_grad(spread_hidden, second_blocks, crossed, True)
    crossed = swap(pack(first_blocks, [token]), "slab", 1)
    first_grad, _ = weight_grad(spread_in, first_blocks, crossed, False)
    return jnp.transpose(first_grad, (0, 2, 1)), jnp.transpose(second_grad, (0, 2, 1))


def solution(mesh):
    placed = (
        P("slab", "filt", None),
        P(None, "filt", None),
        P(None, "filt", None),
        P(None, "filt"),
        P("slab", None),
    )
    return jax.shard_map(
        shards,
        mesh=mesh,
        in_specs=placed,
        out_specs=(P(None, "filt", "slab"), P(None, "filt", "slab")),
        check_vma=False,
    )
```

profile of v0, /device:TPU:0, one launch (start us, length us, event | category | flops | bytes accessed | tf_op | source)
XLA Modules:
  0.0 109.5 jit_solution(10448275260757546131)
XLA Ops:
  0.6 3.0 %collective-permute-start = (bf16[2,128,256]{2,1,0:T(8,128)(2,1)}, bf16[2,128,256]{2,1,0:T(8,128)(2,1)S(1)}, u32[]{:S(2)}, u32[]{:S(2)}) collective-permute-start(bf16[2,128,256]{2,1,0:T(8,128)(2,1)} %refs_0_.2), channel_id=1, source_target_pairs={{0,1},{1,0},{2,3},{3,2},{4,5},{5,4},{6,7},{7,6},{8,9},{9,8},{10,11... | collective-permute-start | bytes 393224 | tf_op jit(solution)/shard_map/ppermute | solution.py:19
  3.6 1.5 %collective-permute-start.1 = (bf16[2,128,256]{2,1,0:T(8,128)(2,1)}, bf16[2,128,256]{2,1,0:T(8,128)(2,1)S(1)}, u32[]{:S(2)}, u32[]{:S(2)}) collective-permute-start(bf16[2,128,256]{2,1,0:T(8,128)(2,1)} %refs_0_.2), channel_id=1, source_target_pairs={{0,2},{1,3},{2,0},{3,1},{4,6},{5,7},{6,4},{7,5},{8,10},{9,11},{10,... | collective-permute-start | bytes 393224 | tf_op jit(solution)/shard_map/ppermute | solution.py:19
  5.2 2.0 %copy-done.1 = bf16[27,128,512]{2,1,0:T(8,128)(2,1)S(1)} copy-done((bf16[27,128,512]{2,1,0:T(8,128)(2,1)S(1)}, bf16[27,128,512]{2,1,0:T(8,128)(2,1)}, u32[]{:S(2)}) %copy-start.1) | copy-done | bytes 3538968
  9.3 2.3 %collective-permute-done.1.refs_2_ = bf16[2,128,256]{2,1,0:T(8,128)(2,1)S(1)} collective-permute-done((bf16[2,128,256]{2,1,0:T(8,128)(2,1)}, bf16[2,128,256]{2,1,0:T(8,128)(2,1)S(1)}, u32[]{:S(2)}, u32[]{:S(2)}) %collective-permute-start.1) | collective-permute-done | bytes 131104 | tf_op jit(solution)/shard_map/ppermute | solution.py:19
  11.8 1.6 %collective-permute-start.3 = (bf16[2,2,32,256]{3,2,1,0:T(8,128)(2,1)S(1)}, bf16[2,2,32,256]{3,2,1,0:T(8,128)(2,1)S(1)}, u32[]{:S(2)}, u32[]{:S(2)}) collective-permute-start(bf16[2,2,32,256]{3,2,1,0:T(8,128)(2,1)S(1)} %get-tuple-element.32), channel_id=1, source_target_pairs={{0,8},{4,12},{8,0},{12,4},{16,24},{20,28},{24,16},{28,20},{1,9},{5... | collective-permute-start | bytes 196616 | tf_op jit(solution)/shard_map/ppermute | solution.py:19
  13.4 2.6 %collective-permute-start.4 = (bf16[2,2,32,256]{3,2,1,0:T(8,128)(2,1)S(1)}, bf16[2,2,32,256]{3,2,1,0:T(8,128)(2,1)S(1)}, u32[]{:S(2)}, u32[]{:S(2)}) collective-permute-start(bf16[2,2,32,256]{3,2,1,0:T(8,128)(2,1)S(1)} %get-tuple-element.33), channel_id=1, source_target_pairs={{0,16},{4,20},{8,24},{12,28},{16,0},{20,4},{24,8},{28,12},{1,17},{... | collective-permute-start | bytes 196616 | tf_op jit(solution)/shard_map/ppermute | solution.py:19
  16.2 1.7 %shard_map.70.refs_1_.refs_2_ = f32[2,128,256]{2,1,0:T(8,128)S(1)} custom-call(bf16[2,512,256]{2,1,0:T(8,128)(2,1)S(1)} %get-tuple-element.35.refs_0_, bf16[27,128,512]{2,1,0:T(8,128)(2,1)S(1)} %get-tuple-element.36.refs_1_), custom_call_target="tpu_custom_call" | custom-call | flops 1207959552 | bytes 3538944 | tf_op jit(solution)/shard_map/pallas_call | solution.py:56
  17.9 3.2 %collective-permute-done.4.refs_3_.refs_2_ = bf16[2,2,32,256]{3,2,1,0:T(8,128)(2,1)S(1)} collective-permute-done((bf16[2,2,32,256]{3,2,1,0:T(8,128)(2,1)S(1)}, bf16[2,2,32,256]{3,2,1,0:T(8,128)(2,1)S(1)}, u32[]{:S(2)}, u32[]{:S(2)}) %collective-permute-start.4) | collective-permute-done | bytes 65568 | tf_op jit(solution)/shard_map/ppermute | solution.py:19
  22.1 3.1 %collective-permute-start.7 = (bf16[1,512,256]{2,1,0:T(8,128)(2,1)S(1)}, bf16[1,512,256]{2,1,0:T(8,128)(2,1)S(1)}, u32[]{:S(2)}, u32[]{:S(2)}) collective-permute-start(bf16[1,512,256]{2,1,0:T(8,128)(2,1)S(1)} %shard_map.71), channel_id=1, source_target_pairs={{0,8},{8,16},{16,24},{12,4},{20,12},{28,20},{1,9},{9,17},{17,25},{... | collective-permute-start | bytes 786440 | tf_op jit(solution)/shard_map/ppermute | solution.py:31
  25.9 3.3 %collective-permute-done.7.refs_0_ = bf16[1,512,256]{2,1,0:T(8,128)(2,1)S(1)} collective-permute-done((bf16[1,512,256]{2,1,0:T(8,128)(2,1)S(1)}, bf16[1,512,256]{2,1,0:T(8,128)(2,1)S(1)}, u32[]{:S(2)}, u32[]{:S(2)}) %collective-permute-start.7) | collective-permute-done | bytes 262176 | tf_op jit(solution)/shard_map/ppermute | solution.py:31
  33.6 2.8 %collective-permute-done.10.refs_1_ = bf16[2,128,256]{2,1,0:T(8,128)(2,1)S(1)} collective-permute-done((bf16[2,128,256]{2,1,0:T(8,128)(2,1)S(1)}, bf16[2,128,256]{2,1,0:T(8,128)(2,1)S(1)}, u32[]{:S(2)}, u32[]{:S(2)}) %collective-permute-start.10) | collective-permute-done | bytes 131104 | tf_op jit(solution)/shard_map/ppermute | solution.py:19
  36.3 1.7 %collective-permute-done.11.refs_2_ = bf16[2,128,256]{2,1,0:T(8,128)(2,1)S(1)} collective-permute-done((bf16[2,128,256]{2,1,0:T(8,128)(2,1)S(1)}, bf16[2,128,256]{2,1,0:T(8,128)(2,1)S(1)}, u32[]{:S(2)}, u32[]{:S(2)}) %collective-permute-start.11) | collective-permute-done | bytes 131104 | tf_op jit(solution)/shard_map/ppermute | solution.py:19
  38.0 1.6 %collective-permute-done.12.refs_3_ = bf16[2,128,256]{2,1,0:T(8,128)(2,1)S(1)} collective-permute-done((bf16[2,128,256]{2,1,0:T(8,128)(2,1)S(1)}, bf16[2,128,256]{2,1,0:T(8,128)(2,1)S(1)}, u32[]{:S(2)}, u32[]{:S(2)}) %collective-permute-start.12) | collective-permute-done | bytes 131104 | tf_op jit(solution)/shard_map/ppermute | solution.py:19
  40.7 2.5 %collective-permute-start.14 = (bf16[2,2,32,256]{3,2,1,0:T(8,128)(2,1)S(1)}, bf16[2,2,32,256]{3,2,1,0:T(8,128)(2,1)S(1)}, u32[]{:S(2)}, u32[]{:S(2)}) collective-permute-start(bf16[2,2,32,256]{3,2,1,0:T(8,128)(2,1)S(1)} %get-tuple-element.42), channel_id=1, source_target_pairs={{0,8},{4,12},{8,0},{12,4},{16,24},{20,28},{24,16},{28,20},{1,9},{5... | collective-permute-start | bytes 196616 | tf_op jit(solution)/shard_map/ppermute | solution.py:19
  43.2 1.7 %collective-permute-start.15 = (bf16[2,2,32,256]{3,2,1,0:T(8,128)(2,1)S(1)}, bf16[2,2,32,256]{3,2,1,0:T(8,128)(2,1)S(1)}, u32[]{:S(2)}, u32[]{:S(2)}) collective-permute-start(bf16[2,2,32,256]{3,2,1,0:T(8,128)(2,1)S(1)} %get-tuple-element.43), channel_id=1, source_target_pairs={{0,16},{4,20},{8,24},{12,28},{16,0},{20,4},{24,8},{28,12},{1,17},{... | collective-permute-start | bytes 196616 | tf_op jit(solution)/shard_map/ppermute | solution.py:19
  45.5 1.7 %shard_map.78.refs_1_.refs_2_ = f32[2,128,256]{2,1,0:T(8,128)S(1)} custom-call(bf16[2,512,256]{2,1,0:T(8,128)(2,1)S(1)} %get-tuple-element.41.refs_0_, bf16[27,128,512]{2,1,0:T(8,128)(2,1)S(1)} %copy-done), custom_call_target="tpu_custom_call" | custom-call | flops 1207959552 | bytes 3538944 | tf_op jit(solution)/shard_map/pallas_call | solution.py:56
  47.3 4.1 %collective-permute-done.15.refs_3_.refs_2_ = bf16[2,2,32,256]{3,2,1,0:T(8,128)(2,1)S(1)} collective-permute-done((bf16[2,2,32,256]{3,2,1,0:T(8,128)(2,1)S(1)}, bf16[2,2,32,256]{3,2,1,0:T(8,128)(2,1)S(1)}, u32[]{:S(2)}, u32[]{:S(2)}) %collective-permute-start.15) | collective-permute-done | bytes 65568 | tf_op jit(solution)/shard_map/ppermute | solution.py:19
  51.4 3.2 %collective-permute-start.17 = (bf16[1,512,256]{2,1,0:T(8,128)(2,1)S(1)}, bf16[1,512,256]{2,1,0:T(8,128)(2,1)S(1)}, u32[]{:S(2)}, u32[]{:S(2)}) collective-permute-start(bf16[1,512,256]{2,1,0:T(8,128)(2,1)S(1)} %shard_map.79), channel_id=1, source_target_pairs={{0,8},{8,16},{16,24},{12,4},{20,12},{28,20},{1,9},{9,17},{17,25},{... | collective-permute-start | bytes 786440 | tf_op jit(solution)/shard_map/ppermute | solution.py:31
  55.3 3.3 %collective-permute-done.17.refs_0_ = bf16[1,512,256]{2,1,0:T(8,128)(2,1)S(1)} collective-permute-done((bf16[1,512,256]{2,1,0:T(8,128)(2,1)S(1)}, bf16[1,512,256]{2,1,0:T(8,128)(2,1)S(1)}, u32[]{:S(2)}, u32[]{:S(2)}) %collective-permute-start.17) | collective-permute-done | bytes 262176 | tf_op jit(solution)/shard_map/ppermute | solution.py:31
  64.5 1.7 %collective-permute-done.20.refs_6_ = f32[2,8,256]{2,1,0:T(8,128)S(1)} collective-permute-done((f32[2,8,256]{2,1,0:T(8,128)S(1)}, f32[2,8,256]{2,1,0:T(8,128)S(1)}, u32[]{:S(2)}, u32[]{:S(2)}) %collective-permute-start.20) | collective-permute-done | bytes 16416 | tf_op jit(solution)/shard_map/ppermute | solution.py:19
  66.6 1.6 %collective-permute-start.24 = (bf16[16,32,256]{2,1,0:T(8,128)(2,1)S(1)}, bf16[16,32,256]{2,1,0:T(8,128)(2,1)S(1)}, u32[]{:S(2)}, u32[]{:S(2)}) collective-permute-start(bf16[16,32,256]{2,1,0:T(8,128)(2,1)S(1)} %shard_map.87.refs_3_.refs_0_), channel_id=1, source_target_pairs={{0,1},{1,0},{2,3},{3,2},{4,5},{5,4},{6,7},{7,6},{8,9},{9,8},{10,11... | collective-permute-start | bytes 786440 | tf_op jit(solution)/shard_map/ppermute | solution.py:19
  68.1 3.4 %collective-permute-start.25 = (bf16[2,256,128]{2,1,0:T(8,128)(2,1)S(1)}, bf16[2,256,128]{2,1,0:T(8,128)(2,1)S(1)}, u32[]{:S(2)}, u32[]{:S(2)}) collective-permute-start(bf16[2,256,128]{2,1,0:T(8,128)(2,1)S(1)} %shard_map.82.refs_0_.refs_5_.refs_2_), channel_id=1, source_target_pairs={{0,16},{4,20},{8,24},{12,28},{16,0},{20,4},{24,8},{28,12},{1,17},{... | collective-permute-start | bytes 393224 | tf_op jit(solution)/shard_map/ppermute | solution.py:19
  71.5 1.6 %shard_map.83.refs_1_.refs_2_ = f32[2,256,512]{2,1,0:T(8,128)S(1)} custom-call(bf16[2,256,128]{2,1,0:T(8,128)(2,1)S(1)} %shard_map.82.refs_0_.refs_5_.refs_2_, bf16[27,128,512]{2,1,0:T(8,128)(2,1)S(1)} %copy-done), custom_call_target="tpu_custom_call" | custom-call | flops 1207959552 | bytes 3538944 | tf_op jit(solution)/shard_map/pallas_call | solution.py:56
  73.1 2.5 %collective-permute-start.22 = (bf16[1,256,128]{2,1,0:T(8,128)(2,1)S(1)}, bf16[1,256,128]{2,1,0:T(8,128)(2,1)S(1)}, u32[]{:S(2)}, u32[]{:S(2)}) collective-permute-start(bf16[1,256,128]{2,1,0:T(8,128)(2,1)S(1)} %shard_map.84), channel_id=1, source_target_pairs={{0,8},{8,16},{16,24},{12,4},{20,12},{28,20},{1,9},{9,17},{17,25},{... | collective-permute-start | bytes 196616 | tf_op jit(solution)/shard_map/ppermute | solution.py:31
  75.8 2.8 %collective-permute-done.25.refs_5_.refs_8_.refs_1_ = bf16[2,256,128]{2,1,0:T(8,128)(2,1)S(1)} collective-permute-done((bf16[2,256,128]{2,1,0:T(8,128)(2,1)S(1)}, bf16[2,256,128]{2,1,0:T(8,128)(2,1)S(1)}, u32[]{:S(2)}, u32[]{:S(2)}) %collective-permute-start.25) | collective-permute-done | bytes 131104 | tf_op jit(solution)/shard_map/ppermute | solution.py:19
  81.7 1.7 %collective-permute-start.28 = (bf16[2,256,128]{2,1,0:T(8,128)(2,1)S(1)}, bf16[2,256,128]{2,1,0:T(8,128)(2,1)S(1)}, u32[]{:S(2)}, u32[]{:S(2)}) collective-permute-start(bf16[2,256,128]{2,1,0:T(8,128)(2,1)S(1)} %get-tuple-element.51), channel_id=1, source_target_pairs={{0,3},{1,2},{2,1},{3,0},{4,7},{5,6},{6,5},{7,4},{8,11},{9,10},{10,... | collective-permute-start | bytes 393224 | tf_op jit(solution)/shard_map/ppermute | solution.py:19
  86.3 1.9 %collective-permute-done.27.refs_3_ = bf16[2,256,128]{2,1,0:T(8,128)(2,1)S(1)} collective-permute-done((bf16[2,256,128]{2,1,0:T(8,128)(2,1)S(1)}, bf16[2,256,128]{2,1,0:T(8,128)(2,1)S(1)}, u32[]{:S(2)}, u32[]{:S(2)}) %collective-permute-start.27) | collective-permute-done | bytes 131104 | tf_op jit(solution)/shard_map/ppermute | solution.py:19
  88.5 2.1 %collective-permute-start.31 = (bf16[2,256,128]{2,1,0:T(8,128)(2,1)S(1)}, bf16[2,256,128]{2,1,0:T(8,128)(2,1)S(1)}, u32[]{:S(2)}, u32[]{:S(2)}) collective-permute-start(bf16[2,256,128]{2,1,0:T(8,128)(2,1)S(1)} %shard_map.90.refs_3_.refs_0_.refs_2_), channel_id=1, source_target_pairs={{0,8},{4,12},{8,0},{12,4},{16,24},{20,28},{24,16},{28,20},{1,9},{5... | collective-permute-start | bytes 393224 | tf_op jit(solution)/shard_map/ppermute | solution.py:19
  93.0 4.0 %shard_map.92 = (f32[27,64,128]{2,1,0:T(8,128)}, f32[8,128]{1,0:T(8,128)S(1)}) custom-call(bf16[576,4096]{1,0:T(8,128)(2,1)S(1)} %get-tuple-element.54.refs_0_, bf16[768,256]{1,0:T(8,128)(2,1)S(1)} %collective-permute-done.34.refs_1_, bf16[2,256,128]{2,1,0:T(8,128)(2,1)S(1)} %shard_map.82.refs_0_.refs_5_.refs_2_, ...), custom_call_target="tpu_custom_call" | custom-call | flops 1811939328 | bytes 5603328 | tf_op jit(solution)/shard_map/pallas_call | solution.py:56
  97.0 6.5 %collective-permute-done.32.refs_2_.refs_4_ = bf16[2,256,128]{2,1,0:T(8,128)(2,1)S(1)} collective-permute-done((bf16[2,256,128]{2,1,0:T(8,128)(2,1)S(1)}, bf16[2,256,128]{2,1,0:T(8,128)(2,1)S(1)}, u32[]{:S(2)}, u32[]{:S(2)}) %collective-permute-start.32) | collective-permute-done | bytes 131104 | tf_op jit(solution)/shard_map/ppermute | solution.py:19
  103.7 1.9 %collective-permute-done.35.refs_1_ = bf16[1024,256]{1,0:T(8,128)(2,1)S(1)} collective-permute-done((bf16[1024,256]{1,0:T(8,128)(2,1)S(1)}, bf16[1024,256]{1,0:T(8,128)(2,1)S(1)}, u32[]{:S(2)}, u32[]{:S(2)}) %collective-permute-start.35) | collective-permute-done | bytes 524320 | tf_op jit(solution)/shard_map/ppermute | solution.py:19
  105.6 3.9 %shard_map.94 = (f32[27,64,128]{2,1,0:T(8,128)}, f32[8,128]{1,0:T(8,128)}) custom-call(bf16[576,4096]{1,0:T(8,128)(2,1)S(1)} %get-tuple-element.38.refs_0_, bf16[1024,256]{1,0:T(8,128)(2,1)S(1)} %collective-permute-done.35.refs_1_, bf16[2,256,128]{2,1,0:T(8,128)(2,1)S(1)} %shard_map.90.refs_3_.refs_0_.refs_2_, ...), custom_call_target="tpu_custom_call" | custom-call | flops 1811939328 | bytes 5603328 | tf_op jit(solution)/shard_map/pallas_call | solution.py:56
  (77 shorter events, 26.0 us)
Async XLA Ops:
  0.6 8.7 %collective-permute-start = (bf16[2,128,256]{2,1,0:T(8,128)(2,1)}, bf16[2,128,256]{2,1,0:T(8,128)(2,1)S(1)}, u32[]{:S(2)}, u32[]{:S(2)}) collective-permute-start(bf16[2,128,256]{2,1,0:T(8,128)(2,1)} %refs_0_.2), channel_id=1, source_target_pairs={{0,1},{1,0},{2,3},{3,2},{4,5},{5,4},{6,7},{7,6},{8,9},{9,8},{10,11... | collective-permute-start | bytes 393224 | tf_op jit(solution)/shard_map/ppermute | solution.py:19
  3.6 8.0 %collective-permute-start.1 = (bf16[2,128,256]{2,1,0:T(8,128)(2,1)}, bf16[2,128,256]{2,1,0:T(8,128)(2,1)S(1)}, u32[]{:S(2)}, u32[]{:S(2)}) collective-permute-start(bf16[2,128,256]{2,1,0:T(8,128)(2,1)} %refs_0_.2), channel_id=1, source_target_pairs={{0,2},{1,3},{2,0},{3,1},{4,6},{5,7},{6,4},{7,5},{8,10},{9,11},{10,... | collective-permute-start | bytes 393224 | tf_op jit(solution)/shard_map/ppermute | solution.py:19
  5.2 6.5 %collective-permute-start.2 = (bf16[2,128,256]{2,1,0:T(8,128)(2,1)}, bf16[2,128,256]{2,1,0:T(8,128)(2,1)S(1)}, u32[]{:S(2)}, u32[]{:S(2)}) collective-permute-start(bf16[2,128,256]{2,1,0:T(8,128)(2,1)} %refs_0_.2), channel_id=1, source_target_pairs={{0,3},{1,2},{2,1},{3,0},{4,7},{5,6},{6,5},{7,4},{8,11},{9,10},{10,... | collective-permute-start | bytes 393224 | tf_op jit(solution)/shard_map/ppermute | solution.py:19
  11.7 10.4 %collective-permute-start.6 = (bf16[2,512,256]{2,1,0:T(8,128)(2,1)S(1)}, bf16[2,512,256]{2,1,0:T(8,128)(2,1)S(1)}, u32[]{:S(2)}, u32[]{:S(2)}) collective-permute-start(bf16[2,512,256]{2,1,0:T(8,128)(2,1)S(1)} %get-tuple-element.35.refs_0_), channel_id=1, source_target_pairs={{0,4},{4,0},{8,12},{12,8},{16,20},{20,16},{24,28},{28,24},{1,5},{5... | collective-permute-start | bytes 1572872 | tf_op jit(solution)/shard_map/ppermute | solution.py:19
  11.8 6.2 %collective-permute-start.3 = (bf16[2,2,32,256]{3,2,1,0:T(8,128)(2,1)S(1)}, bf16[2,2,32,256]{3,2,1,0:T(8,128)(2,1)S(1)}, u32[]{:S(2)}, u32[]{:S(2)}) collective-permute-start(bf16[2,2,32,256]{3,2,1,0:T(8,128)(2,1)S(1)} %get-tuple-element.32), channel_id=1, source_target_pairs={{0,8},{4,12},{8,0},{12,4},{16,24},{20,28},{24,16},{28,20},{1,9},{5... | collective-permute-start | bytes 196616 | tf_op jit(solution)/shard_map/ppermute | solution.py:19
  13.4 7.7 %collective-permute-start.4 = (bf16[2,2,32,256]{3,2,1,0:T(8,128)(2,1)S(1)}, bf16[2,2,32,256]{3,2,1,0:T(8,128)(2,1)S(1)}, u32[]{:S(2)}, u32[]{:S(2)}) collective-permute-start(bf16[2,2,32,256]{3,2,1,0:T(8,128)(2,1)S(1)} %get-tuple-element.33), channel_id=1, source_target_pairs={{0,16},{4,20},{8,24},{12,28},{16,0},{20,4},{24,8},{28,12},{1,17},{... | collective-permute-start | bytes 196616 | tf_op jit(solution)/shard_map/ppermute | solution.py:19
  16.0 6.1 %collective-permute-start.5 = (bf16[2,2,32,256]{3,2,1,0:T(8,128)(2,1)S(1)}, bf16[2,2,32,256]{3,2,1,0:T(8,128)(2,1)S(1)}, u32[]{:S(2)}, u32[]{:S(2)}) collective-permute-start(bf16[2,2,32,256]{3,2,1,0:T(8,128)(2,1)S(1)} %get-tuple-element.34), channel_id=1, source_target_pairs={{0,24},{4,28},{8,16},{12,20},{16,8},{20,12},{24,0},{28,4},{1,25},{... | collective-permute-start | bytes 196616 | tf_op jit(solution)/shard_map/ppermute | solution.py:19
  22.1 7.0 %collective-permute-start.7 = (bf16[1,512,256]{2,1,0:T(8,128)(2,1)S(1)}, bf16[1,512,256]{2,1,0:T(8,128)(2,1)S(1)}, u32[]{:S(2)}, u32[]{:S(2)}) collective-permute-start(bf16[1,512,256]{2,1,0:T(8,128)(2,1)S(1)} %shard_map.71), channel_id=1, source_target_pairs={{0,8},{8,16},{16,24},{12,4},{20,12},{28,20},{1,9},{9,17},{17,25},{... | collective-permute-start | bytes 786440 | tf_op jit(solution)/shard_map/ppermute | solution.py:31
  30.0 6.4 %collective-permute-start.10 = (bf16[2,128,256]{2,1,0:T(8,128)(2,1)S(1)}, bf16[2,128,256]{2,1,0:T(8,128)(2,1)S(1)}, u32[]{:S(2)}, u32[]{:S(2)}) collective-permute-start(bf16[2,128,256]{2,1,0:T(8,128)(2,1)S(1)} %get-tuple-element.37.refs_4_.refs_0_), channel_id=1, source_target_pairs={{0,1},{1,0},{2,3},{3,2},{4,5},{5,4},{6,7},{7,6},{8,9},{9,8},{10,11... | collective-permute-start | bytes 393224 | tf_op jit(solution)/shard_map/ppermute | solution.py:19
  31.3 6.8 %collective-permute-start.11 = (bf16[2,128,256]{2,1,0:T(8,128)(2,1)S(1)}, bf16[2,128,256]{2,1,0:T(8,128)(2,1)S(1)}, u32[]{:S(2)}, u32[]{:S(2)}) collective-permute-start(bf16[2,128,256]{2,1,0:T(8,128)(2,1)S(1)} %get-tuple-element.37.refs_4_.refs_0_), channel_id=1, source_target_pairs={{0,2},{1,3},{2,0},{3,1},{4,6},{5,7},{6,4},{7,5},{8,10},{9,11},{10,... | collective-permute-start | bytes 393224 | tf_op jit(solution)/shard_map/ppermute | solution.py:19
  32.1 7.6 %collective-permute-start.12 = (bf16[2,128,256]{2,1,0:T(8,128)(2,1)S(1)}, bf16[2,128,256]{2,1,0:T(8,128)(2,1)S(1)}, u32[]{:S(2)}, u32[]{:S(2)}) collective-permute-start(bf16[2,128,256]{2,1,0:T(8,128)(2,1)S(1)} %get-tuple-element.37.refs_4_.refs_0_), channel_id=1, source_target_pairs={{0,3},{1,2},{2,1},{3,0},{4,7},{5,6},{6,5},{7,4},{8,11},{9,10},{10,... | collective-permute-start | bytes 393224 | tf_op jit(solution)/shard_map/ppermute | solution.py:19
  39.7 11.7 %collective-permute-start.13 = (bf16[2,512,256]{2,1,0:T(8,128)(2,1)S(1)}, bf16[2,512,256]{2,1,0:T(8,128)(2,1)S(1)}, u32[]{:S(2)}, u32[]{:S(2)}) collective-permute-start(bf16[2,512,256]{2,1,0:T(8,128)(2,1)S(1)} %get-tuple-element.41.refs_0_), channel_id=1, source_target_pairs={{0,4},{4,0},{8,12},{12,8},{16,20},{20,16},{24,28},{28,24},{1,5},{5... | collective-permute-start | bytes 1572872 | tf_op jit(solution)/shard_map/ppermute | solution.py:19
  39.8 15.5 %collective-permute-start.9 = (bf16[16,32,256]{2,1,0:T(8,128)(2,1)S(1)}, bf16[16,32,256]{2,1,0:T(8,128)(2,1)S(1)}, u32[]{:S(2)}, u32[]{:S(2)}) collective-permute-start(bf16[16,32,256]{2,1,0:T(8,128)(2,1)S(1)} %shard_map.75.refs_0_.refs_4_), channel_id=1, source_target_pairs={{0,1},{1,0},{2,3},{3,2},{4,5},{5,4},{6,7},{7,6},{8,9},{9,8},{10,11... | collective-permute-start | bytes 786440 | tf_op jit(solution)/shard_map/ppermute | solution.py:19
  40.7 6.6 %collective-permute-start.14 = (bf16[2,2,32,256]{3,2,1,0:T(8,128)(2,1)S(1)}, bf16[2,2,32,256]{3,2,1,0:T(8,128)(2,1)S(1)}, u32[]{:S(2)}, u32[]{:S(2)}) collective-permute-start(bf16[2,2,32,256]{3,2,1,0:T(8,128)(2,1)S(1)} %get-tuple-element.42), channel_id=1, source_target_pairs={{0,8},{4,12},{8,0},{12,4},{16,24},{20,28},{24,16},{28,20},{1,9},{5... | collective-permute-start | bytes 196616 | tf_op jit(solution)/shard_map/ppermute | solution.py:19
  43.2 8.3 %collective-permute-start.15 = (bf16[2,2,32,256]{3,2,1,0:T(8,128)(2,1)S(1)}, bf16[2,2,32,256]{3,2,1,0:T(8,128)(2,1)S(1)}, u32[]{:S(2)}, u32[]{:S(2)}) collective-permute-start(bf16[2,2,32,256]{3,2,1,0:T(8,128)(2,1)S(1)} %get-tuple-element.43), channel_id=1, source_target_pairs={{0,16},{4,20},{8,24},{12,28},{16,0},{20,4},{24,8},{28,12},{1,17},{... | collective-permute-start | bytes 196616 | tf_op jit(solution)/shard_map/ppermute | solution.py:19
  44.8 6.6 %collective-permute-start.16 = (bf16[2,2,32,256]{3,2,1,0:T(8,128)(2,1)S(1)}, bf16[2,2,32,256]{3,2,1,0:T(8,128)(2,1)S(1)}, u32[]{:S(2)}, u32[]{:S(2)}) collective-permute-start(bf16[2,2,32,256]{3,2,1,0:T(8,128)(2,1)S(1)} %get-tuple-element.44), channel_id=1, source_target_pairs={{0,24},{4,28},{8,16},{12,20},{16,8},{20,12},{24,0},{28,4},{1,25},{... | collective-permute-start | bytes 196616 | tf_op jit(solution)/shard_map/ppermute | solution.py:19
  51.4 7.1 %collective-permute-start.17 = (bf16[1,512,256]{2,1,0:T(8,128)(2,1)S(1)}, bf16[1,512,256]{2,1,0:T(8,128)(2,1)S(1)}, u32[]{:S(2)}, u32[]{:S(2)}) collective-permute-start(bf16[1,512,256]{2,1,0:T(8,128)(2,1)S(1)} %shard_map.79), channel_id=1, source_target_pairs={{0,8},{8,16},{16,24},{12,4},{20,12},{28,20},{1,9},{9,17},{17,25},{... | collective-permute-start | bytes 786440 | tf_op jit(solution)/shard_map/ppermute | solution.py:31
  59.4 7.1 %collective-permute-start.23 = (bf16[8,32,256]{2,1,0:T(8,128)(2,1)S(1)}, bf16[8,32,256]{2,1,0:T(8,128)(2,1)S(1)}, u32[]{:S(2)}, u32[]{:S(2)}) collective-permute-start(bf16[8,32,256]{2,1,0:T(8,128)(2,1)S(1)} %shard_map.86), channel_id=1, source_target_pairs={{0,4},{4,0},{8,12},{12,8},{16,20},{20,16},{24,28},{28,24},{1,5},{5... | collective-permute-start | bytes 393224 | tf_op jit(solution)/shard_map/ppermute | solution.py:19
  61.6 4.6 %collective-permute-start.20 = (f32[2,8,256]{2,1,0:T(8,128)S(1)}, f32[2,8,256]{2,1,0:T(8,128)S(1)}, u32[]{:S(2)}, u32[]{:S(2)}) collective-permute-start(f32[2,8,256]{2,1,0:T(8,128)S(1)} %get-tuple-element.46.refs_3_.refs_4_), channel_id=1, source_target_pairs={{0,3},{1,2},{2,1},{3,0},{4,7},{5,6},{6,5},{7,4},{8,11},{9,10},{10,... | collective-permute-start | bytes 49160 | tf_op jit(solution)/shard_map/ppermute | solution.py:19
  66.6 12.7 %collective-permute-start.24 = (bf16[16,32,256]{2,1,0:T(8,128)(2,1)S(1)}, bf16[16,32,256]{2,1,0:T(8,128)(2,1)S(1)}, u32[]{:S(2)}, u32[]{:S(2)}) collective-permute-start(bf16[16,32,256]{2,1,0:T(8,128)(2,1)S(1)} %shard_map.87.refs_3_.refs_0_), channel_id=1, source_target_pairs={{0,1},{1,0},{2,3},{3,2},{4,5},{5,4},{6,7},{7,6},{8,9},{9,8},{10,11... | collective-permute-start | bytes 786440 | tf_op jit(solution)/shard_map/ppermute | solution.py:19
  68.1 5.0 %collective-permute-start.21 = (bf16[2,256,128]{2,1,0:T(8,128)(2,1)S(1)}, bf16[2,256,128]{2,1,0:T(8,128)(2,1)S(1)}, u32[]{:S(2)}, u32[]{:S(2)}) collective-permute-start(bf16[2,256,128]{2,1,0:T(8,128)(2,1)S(1)} %shard_map.82.refs_0_.refs_5_.refs_2_), channel_id=1, source_target_pairs={{0,4},{4,0},{8,12},{12,8},{16,20},{20,16},{24,28},{28,24},{1,5},{5... | collective-permute-start | bytes 393224 | tf_op jit(solution)/shard_map/ppermute | solution.py:19
  68.1 10.5 %collective-permute-start.25 = (bf16[2,256,128]{2,1,0:T(8,128)(2,1)S(1)}, bf16[2,256,128]{2,1,0:T(8,128)(2,1)S(1)}, u32[]{:S(2)}, u32[]{:S(2)}) collective-permute-start(bf16[2,256,128]{2,1,0:T(8,128)(2,1)S(1)} %shard_map.82.refs_0_.refs_5_.refs_2_), channel_id=1, source_target_pairs={{0,16},{4,20},{8,24},{12,28},{16,0},{20,4},{24,8},{28,12},{1,17},{... | collective-permute-start | bytes 393224 | tf_op jit(solution)/shard_map/ppermute | solution.py:19
  73.1 6.1 %collective-permute-start.22 = (bf16[1,256,128]{2,1,0:T(8,128)(2,1)S(1)}, bf16[1,256,128]{2,1,0:T(8,128)(2,1)S(1)}, u32[]{:S(2)}, u32[]{:S(2)}) collective-permute-start(bf16[1,256,128]{2,1,0:T(8,128)(2,1)S(1)} %shard_map.84), channel_id=1, source_target_pairs={{0,8},{8,16},{16,24},{12,4},{20,12},{28,20},{1,9},{9,17},{17,25},{... | collective-permute-start | bytes 196616 | tf_op jit(solution)/shard_map/ppermute | solution.py:31
  75.6 10.3 %collective-permute-start.29 = (bf16[2,256,128]{2,1,0:T(8,128)(2,1)S(1)}, bf16[2,256,128]{2,1,0:T(8,128)(2,1)S(1)}, u32[]{:S(2)}, u32[]{:S(2)}) collective-permute-start(bf16[2,256,128]{2,1,0:T(8,128)(2,1)S(1)} %shard_map.82.refs_0_.refs_5_.refs_2_), channel_id=1, source_target_pairs={{0,8},{4,12},{8,0},{12,4},{16,24},{20,28},{24,16},{28,20},{1,9},{5... | collective-permute-start | bytes 393224 | tf_op jit(solution)/shard_map/ppermute | solution.py:19
  78.6 7.2 %collective-permute-start.30 = (bf16[2,256,128]{2,1,0:T(8,128)(2,1)S(1)}, bf16[2,256,128]{2,1,0:T(8,128)(2,1)S(1)}, u32[]{:S(2)}, u32[]{:S(2)}) collective-permute-start(bf16[2,256,128]{2,1,0:T(8,128)(2,1)S(1)} %collective-permute-done.25.refs_5_.refs_8_.refs_1_), channel_id=1, source_target_pairs={{0,8},{4,12},{8,0},{12,4},{16,24},{20,28},{24,16},{28,20},{1,9},{5... | collective-permute-start | bytes 393224 | tf_op jit(solution)/shard_map/ppermute | solution.py:19
  79.9 6.5 %collective-permute-start.26 = (bf16[2,256,128]{2,1,0:T(8,128)(2,1)S(1)}, bf16[2,256,128]{2,1,0:T(8,128)(2,1)S(1)}, u32[]{:S(2)}, u32[]{:S(2)}) collective-permute-start(bf16[2,256,128]{2,1,0:T(8,128)(2,1)S(1)} %get-tuple-element.49), channel_id=1, source_target_pairs={{0,1},{1,0},{2,3},{3,2},{4,5},{5,4},{6,7},{7,6},{8,9},{9,8},{10,11... | collective-permute-start | bytes 393224 | tf_op jit(solution)/shard_map/ppermute | solution.py:19
  80.5 7.8 %collective-permute-start.27 = (bf16[2,256,128]{2,1,0:T(8,128)(2,1)S(1)}, bf16[2,256,128]{2,1,0:T(8,128)(2,1)S(1)}, u32[]{:S(2)}, u32[]{:S(2)}) collective-permute-start(bf16[2,256,128]{2,1,0:T(8,128)(2,1)S(1)} %get-tuple-element.50), channel_id=1, source_target_pairs={{0,2},{1,3},{2,0},{3,1},{4,6},{5,7},{6,4},{7,5},{8,10},{9,11},{10,... | collective-permute-start | bytes 393224 | tf_op jit(solution)/shard_map/ppermute | solution.py:19
  81.7 6.6 %collective-permute-start.28 = (bf16[2,256,128]{2,1,0:T(8,128)(2,1)S(1)}, bf16[2,256,128]{2,1,0:T(8,128)(2,1)S(1)}, u32[]{:S(2)}, u32[]{:S(2)}) collective-permute-start(bf16[2,256,128]{2,1,0:T(8,128)(2,1)S(1)} %get-tuple-element.51), channel_id=1, source_target_pairs={{0,3},{1,2},{2,1},{3,0},{4,7},{5,6},{6,5},{7,4},{8,11},{9,10},{10,... | collective-permute-start | bytes 393224 | tf_op jit(solution)/shard_map/ppermute | solution.py:19
  88.4 4.6 %collective-permute-start.34 = (bf16[768,256]{1,0:T(8,128)(2,1)S(1)}, bf16[768,256]{1,0:T(8,128)(2,1)S(1)}, u32[]{:S(2)}, u32[]{:S(2)}) collective-permute-start(bf16[768,256]{1,0:T(8,128)(2,1)S(1)} %shard_map.91), channel_id=1, source_target_pairs={{0,4},{4,0},{8,12},{12,8},{16,20},{20,16},{24,28},{28,24},{1,5},{5... | collective-permute-start | bytes 1179656 | tf_op jit(solution)/shard_map/ppermute | solution.py:19
  88.5 8.5 %collective-permute-start.31 = (bf16[2,256,128]{2,1,0:T(8,128)(2,1)S(1)}, bf16[2,256,128]{2,1,0:T(8,128)(2,1)S(1)}, u32[]{:S(2)}, u32[]{:S(2)}) collective-permute-start(bf16[2,256,128]{2,1,0:T(8,128)(2,1)S(1)} %shard_map.90.refs_3_.refs_0_.refs_2_), channel_id=1, source_target_pairs={{0,8},{4,12},{8,0},{12,4},{16,24},{20,28},{24,16},{28,20},{1,9},{5... | collective-permute-start | bytes 393224 | tf_op jit(solution)/shard_map/ppermute | solution.py:19
  90.6 12.9 %collective-permute-start.32 = (bf16[2,256,128]{2,1,0:T(8,128)(2,1)S(1)}, bf16[2,256,128]{2,1,0:T(8,128)(2,1)S(1)}, u32[]{:S(2)}, u32[]{:S(2)}) collective-permute-start(bf16[2,256,128]{2,1,0:T(8,128)(2,1)S(1)} %shard_map.90.refs_3_.refs_0_.refs_2_), channel_id=1, source_target_pairs={{0,16},{4,20},{8,24},{12,28},{16,0},{20,4},{24,8},{28,12},{1,17},{... | collective-permute-start | bytes 393224 | tf_op jit(solution)/shard_map/ppermute | solution.py:19
  92.0 11.5 %collective-permute-start.33 = (bf16[2,256,128]{2,1,0:T(8,128)(2,1)S(1)}, bf16[2,256,128]{2,1,0:T(8,128)(2,1)S(1)}, u32[]{:S(2)}, u32[]{:S(2)}) collective-permute-start(bf16[2,256,128]{2,1,0:T(8,128)(2,1)S(1)} %shard_map.90.refs_3_.refs_0_.refs_2_), channel_id=1, source_target_pairs={{0,24},{4,28},{8,16},{12,20},{16,8},{20,12},{24,0},{28,4},{1,25},{... | collective-permute-start | bytes 393224 | tf_op jit(solution)/shard_map/ppermute | solution.py:19
  (9 other events, 47.4 us)
where the time goes:
time: 110 us; the launch traced here: 109 us
  starting transfers between devices  44.4 us (40%)
  waiting for transfers between devices  40.1 us (36%)
  Pallas kernels  20.4 us (19%)
  local copies, waits for them, and re-layouts  3.6 us (3%)
    ppermute x33, starting transfers between devices, swap(): return lax.ppermute(block, axis, [(i, i ^ step) for i in range(count)])  35.6 us
    ppermute x33, waiting for transfers between devices, swap(): return lax.ppermute(block, axis, [(i, i ^ step) for i in range(count)])  33.5 us
    pallas_call x27, Pallas kernels, call(): pl.pallas_call(inner, out_shape=[*outs, *(struct(array.shape, array.dtype...  20.4 us
    ppermute x3, starting transfers between devices, halo(): return (other, lax.ppermute(passed, 'slab', pairs))  8.83 us
    ppermute x3, waiting for transfers between devices, halo(): return (other, lax.ppermute(passed, 'slab', pairs))  6.56 us
    unnamed x10, local copies, waits for them, and re-layouts  3.6 us
  transfers between devices with their start and end apart: 36, of which 17 were waited for; matrix products, arithmetic and copies ran while one was open for 0% of the time, Pallas kernels for 13%

commit v1 on v0

--- a/solution.py
+++ b/solution.py
@@ -20,19 +20,23 @@
 
 
 def exchanged(block, axis):
-    return [block] + [swap(block, axis, step) for step in range(1, lax.axis_size(axis))]
-
-
-def halo(volume, own, due=()):
+    return swapped([block] * lax.axis_size(axis), axis, 1)
+
+
+def swapped(blocks, axis, unit):
+    return [blocks[0]] + [swap(blocks[step], axis, unit * step) for step in range(1, len(blocks))]
+
+
+def halo(volume, own):
     count = lax.axis_size("slab")
     other = swap(volume, "slab", 1)
-    passed = edge(other, [own, *due])
+    passed = edge(other, [own])
     pairs = [(i, i + 2) for i in range(0, count - 2, 2)] + [(i, i - 2) for i in range(3, count, 2)]
     return other, lax.ppermute(passed, "slab", pairs)
 
 
 def chips_apart(blocks):
-    return [swap(block, "slab", 2 + 2 * number) for number, block in enumerate(blocks)]
+    return swapped([None, *blocks], "slab", 2)[1:]
 
 
 def every_chip(block):
@@ -151,7 +155,7 @@
 
 
 def assemble_body(count, split, *refs):
-    parts, whole_ref, shares = refs[:count], refs[count], refs[count + 1 :]
+    parts, whole_ref, shares = refs[:count][::-1], refs[count], refs[count + 1 :]
     size = parts[0].shape[1]
     me, chip = here("filt"), here("slab") // 2
     for step in range(count):
@@ -176,7 +180,7 @@
         functools.partial(assemble_body, count, split),
         outs,
         (0, 4 * planes * channels * plane),
-        *parts,
+        *parts[::-1],
         in_specs=[VMEM] * count,
         after=after,
     )
@@ -227,12 +231,13 @@
 
 def pack_body(count, *refs):
     out_ref = refs[count]
+    blocks = refs[:count][::-1]
     row = 0
     for number in range(count):
-        planes, plane, filters = refs[number].shape
+        planes, plane, filters = blocks[number].shape
         for j in range(planes):
             for begin in range(0, plane, filters):
-                out_ref[row : row + filters, begin : begin + filters] = refs[number][j, begin : begin + filters, :]
+                out_ref[row : row + filters, begin : begin + filters] = blocks[number][j, begin : begin + filters, :]
             row += filters
 
 
@@ -243,7 +248,7 @@
         functools.partial(pack_body, len(blocks)),
         struct((total // plane, plane), blocks[0].dtype),
         (0, 4 * total),
-        *blocks,
+        *blocks[::-1],
         in_specs=[VMEM] * len(blocks),
         after=after,
     )
@@ -344,7 +349,7 @@
 
 
 def loss_body(count, labels_ref, head_ref, slope_ref, *refs):
-    parts, grad_ref = refs[:count], refs[count]
+    parts, grad_ref = refs[:count][::-1], refs[count]
     for j in range(grad_ref.shape[0]):
         logits = parts[0][j]
         for part in parts[1:]:
@@ -369,7 +374,7 @@
         functools.partial(loss_body, len(parts)),
         struct((planes, plane, slope.shape[1]), jnp.bfloat16),
         (2 * slope.size * head.shape[0], slope.size * 6),
-        labels, head, slope, *parts,
+        labels, head, slope, *parts[::-1],
         in_specs=[VMEM] * (3 + len(parts)),
         after=after,
     )
@@ -466,7 +471,7 @@
 
 
 def first_grad_body(count, slope_ref, *refs):
-    parts, out_ref = refs[:count], refs[count]
+    parts, out_ref = refs[:count][::-1], refs[count]
     for j in range(out_ref.shape[0]):
         total = parts[0][j]
         for part in parts[1:]:
@@ -479,7 +484,7 @@
         functools.partial(first_grad_body, len(parts)),
         struct(slope.shape, jnp.bfloat16),
         (slope.size * 4, slope.size * 14),
-        slope, *parts,
+        slope, *parts[::-1],
         in_specs=[VMEM] * (1 + len(parts)),
         after=after,
     )
@@ -570,18 +575,18 @@
     all_in, share_in = assemble([near] + exchanged(features, "filt")[1:])
     own = forward_own(all_in, first_weight)
     share_in = [share_in[0]] + chips_apart(share_in[1:])
-    other, beyond = halo(all_in, own, share_in[1:])
+    other, beyond = halo(all_in, own)
     own = forward_other(other, first_weight, own)
-    slope_first, hidden = forward_rest(beyond, first_weight, own, [])
+    slope_first, hidden = forward_rest(beyond, first_weight, own, share_in[:0:-1])
 
     halved_in = collected(share_in, [hidden])
     all_hidden, share_hidden = assemble(exchanged(hidden, "filt"), [halved_in])
     own = forward_own(all_hidden, second_weight)
     share_hidden = [share_hidden[0]] + chips_apart(share_hidden[1:])
-    other, beyond = halo(all_hidden, own, share_hidden[1:])
+    other, beyond = halo(all_hidden, own)
     own = forward_other(other, second_weight, own)
     halved_in = both_halves(halved_in, split)
-    slope_second, logits = forward_rest(beyond, second_weight, own, halved_in, head_weight)
+    slope_second, logits = forward_rest(beyond, second_weight, own, share_hidden[:0:-1] + halved_in, head_weight)
 
     logits_parts = exchanged(logits, "filt")
     second_out = loss_grad(logits_parts, labels, head_weight, slope_second, [])
@@ -592,7 +597,7 @@
     own = backward_other(second_other, second_weight, own)
     due = halved_hidden + second_far[chips // 2 - 1 : chips // 2]
     kept, *sent = backward_rest(beyond, second_weight, own, count, due)
-    parts = [kept] + [swap(part, "filt", 1 + number) for number, part in enumerate(sent)]
+    parts = swapped([kept, *sent], "filt", 1)
     spread_in, token_in = spread(halved_in)
     spread_hidden, token_hidden = spread(halved_hidden)
     first_out_grad = first_out(parts, slope_first, [token_in, token_hidden, *second_far])

time: 110 us -> 106 us (0.964)
  waiting for transfers between devices: 40.1 us -> 35.5 us
    ppermute x3, waiting for transfers between devices: 6.56 us -> 0.01 us  [halo(): return (other, lax.ppermute(passed, 'slab', pairs))]
    ppermute x3, starting transfers between devices: 8.83 us -> 11.1 us  [halo(): return (other, lax.ppermute(passed, 'slab', pairs))]
    ppermute x33, waiting for transfers between devices: 33.5 us -> 35.5 us  [swap(): return lax.ppermute(block, axis, [(i, i ^ step) for i in range(count)])]
    ppermute x33, starting transfers between devices: 35.6 us -> 33.8 us  [swap(): return lax.ppermute(block, axis, [(i, i ^ step) for i in range(count)])]
  transfers between devices with their start and end apart: 36 -> 36, of which waited for: 17 -> 18; matrix products, arithmetic and copies ran while one was open for 0% -> 0% of each run, Pallas kernels for 13% -> 14%
where the time goes in v1:
time: 106 us; the launch traced here: 105 us
  starting transfers between devices  44.9 us (42%)
  waiting for transfers between devices  35.5 us (33%)
  Pallas kernels  20.4 us (19%)
  local copies, waits for them, and re-layouts  3.6 us (3%)
    ppermute x33, waiting for transfers between devices, swap(): return lax.ppermute(block, axis, [(i, i ^ step) for i in range(count)])  35.5 us
    ppermute x33, starting transfers between devices, swap(): return lax.ppermute(block, axis, [(i, i ^ step) for i in range(count)])  33.8 us
    pallas_call x27, Pallas kernels, call(): pl.pallas_call(inner, out_shape=[*outs, *(struct(array.shape, array.dtype...  20.4 us
    ppermute x3, starting transfers between devices, halo(): return (other, lax.ppermute(passed, 'slab', pairs))  11.1 us
    unnamed x10, local copies, waits for them, and re-layouts  3.6 us
  transfers between devices with their start and end apart: 36, of which 18 were waited for; matrix products, arithmetic and copies ran while one was open for 0% of the time, Pallas kernels for 14%

profile of v1, /device:TPU:0, one launch (start us, length us, event | category | flops | bytes accessed | tf_op | source)
XLA Modules:
  0.0 105.4 jit_solution(1363506226662308735)
XLA Ops:
  0.6 4.0 %collective-permute-start = (bf16[2,128,256]{2,1,0:T(8,128)(2,1)}, bf16[2,128,256]{2,1,0:T(8,128)(2,1)S(1)}, u32[]{:S(2)}, u32[]{:S(2)}) collective-permute-start(bf16[2,128,256]{2,1,0:T(8,128)(2,1)} %refs_0_.2), channel_id=1, source_target_pairs={{0,3},{1,2},{2,1},{3,0},{4,7},{5,6},{6,5},{7,4},{8,11},{9,10},{10,... | collective-permute-start | bytes 393224 | tf_op jit(solution)/shard_map/ppermute | solution.py:19
  5.2 2.0 %copy-done.1 = bf16[27,128,512]{2,1,0:T(8,128)(2,1)S(1)} copy-done((bf16[27,128,512]{2,1,0:T(8,128)(2,1)S(1)}, bf16[27,128,512]{2,1,0:T(8,128)(2,1)}, u32[]{:S(2)}) %copy-start.1) | copy-done | bytes 3538968
  9.4 1.7 %collective-permute-done.1.refs_1_ = bf16[2,128,256]{2,1,0:T(8,128)(2,1)S(1)} collective-permute-done((bf16[2,128,256]{2,1,0:T(8,128)(2,1)}, bf16[2,128,256]{2,1,0:T(8,128)(2,1)S(1)}, u32[]{:S(2)}, u32[]{:S(2)}) %collective-permute-start.1) | collective-permute-done | bytes 131104 | tf_op jit(solution)/shard_map/ppermute | solution.py:19
  11.5 1.7 %shard_map.70.refs_1_.refs_2_ = f32[2,128,256]{2,1,0:T(8,128)S(1)} custom-call(bf16[2,512,256]{2,1,0:T(8,128)(2,1)S(1)} %get-tuple-element.35.refs_0_, bf16[27,128,512]{2,1,0:T(8,128)(2,1)S(1)} %get-tuple-element.36.refs_1_), custom_call_target="tpu_custom_call" | custom-call | flops 1207959552 | bytes 3538944 | tf_op jit(solution)/shard_map/pallas_call | solution.py:60
  13.4 3.5 %collective-permute-start.7 = (bf16[1,512,256]{2,1,0:T(8,128)(2,1)S(1)}, bf16[1,512,256]{2,1,0:T(8,128)(2,1)S(1)}, u32[]{:S(2)}, u32[]{:S(2)}) collective-permute-start(bf16[1,512,256]{2,1,0:T(8,128)(2,1)S(1)} %shard_map.71), channel_id=1, source_target_pairs={{0,8},{8,16},{16,24},{12,4},{20,12},{28,20},{1,9},{9,17},{17,25},{... | collective-permute-start | bytes 786440 | tf_op jit(solution)/shard_map/ppermute | solution.py:35
  16.9 1.6 %collective-permute-start.3 = (bf16[2,2,32,256]{3,2,1,0:T(8,128)(2,1)S(1)}, bf16[2,2,32,256]{3,2,1,0:T(8,128)(2,1)S(1)}, u32[]{:S(2)}, u32[]{:S(2)}) collective-permute-start(bf16[2,2,32,256]{3,2,1,0:T(8,128)(2,1)S(1)} %get-tuple-element.32), channel_id=1, source_target_pairs={{0,8},{4,12},{8,0},{12,4},{16,24},{20,28},{24,16},{28,20},{1,9},{5... | collective-permute-start | bytes 196616 | tf_op jit(solution)/shard_map/ppermute | solution.py:19
  19.6 1.7 %collective-permute-start.5 = (bf16[2,2,32,256]{3,2,1,0:T(8,128)(2,1)S(1)}, bf16[2,2,32,256]{3,2,1,0:T(8,128)(2,1)S(1)}, u32[]{:S(2)}, u32[]{:S(2)}) collective-permute-start(bf16[2,2,32,256]{3,2,1,0:T(8,128)(2,1)S(1)} %get-tuple-element.34), channel_id=1, source_target_pairs={{0,24},{4,28},{8,16},{12,20},{16,8},{20,12},{24,0},{28,4},{1,25},{... | collective-permute-start | bytes 196616 | tf_op jit(solution)/shard_map/ppermute | solution.py:19
  24.3 2.6 %collective-permute-done.5.refs_3_.refs_4_ = bf16[2,2,32,256]{3,2,1,0:T(8,128)(2,1)S(1)} collective-permute-done((bf16[2,2,32,256]{3,2,1,0:T(8,128)(2,1)S(1)}, bf16[2,2,32,256]{3,2,1,0:T(8,128)(2,1)S(1)}, u32[]{:S(2)}, u32[]{:S(2)}) %collective-permute-start.5) | collective-permute-done | bytes 65568 | tf_op jit(solution)/shard_map/ppermute | solution.py:19
  28.0 1.7 %collective-permute-start.10 = (bf16[2,128,256]{2,1,0:T(8,128)(2,1)S(1)}, bf16[2,128,256]{2,1,0:T(8,128)(2,1)S(1)}, u32[]{:S(2)}, u32[]{:S(2)}) collective-permute-start(bf16[2,128,256]{2,1,0:T(8,128)(2,1)S(1)} %get-tuple-element.37.refs_4_.refs_3_), channel_id=1, source_target_pairs={{0,3},{1,2},{2,1},{3,0},{4,7},{5,6},{6,5},{7,4},{8,11},{9,10},{10,... | collective-permute-start | bytes 393224 | tf_op jit(solution)/shard_map/ppermute | solution.py:19
  31.6 3.7 %collective-permute-done.10.refs_0_ = bf16[2,128,256]{2,1,0:T(8,128)(2,1)S(1)} collective-permute-done((bf16[2,128,256]{2,1,0:T(8,128)(2,1)S(1)}, bf16[2,128,256]{2,1,0:T(8,128)(2,1)S(1)}, u32[]{:S(2)}, u32[]{:S(2)}) %collective-permute-start.10) | collective-permute-done | bytes 131104 | tf_op jit(solution)/shard_map/ppermute | solution.py:19
  35.3 2.1 %collective-permute-done.11.refs_1_ = bf16[2,128,256]{2,1,0:T(8,128)(2,1)S(1)} collective-permute-done((bf16[2,128,256]{2,1,0:T(8,128)(2,1)S(1)}, bf16[2,128,256]{2,1,0:T(8,128)(2,1)S(1)}, u32[]{:S(2)}, u32[]{:S(2)}) %collective-permute-start.11) | collective-permute-done | bytes 131104 | tf_op jit(solution)/shard_map/ppermute | solution.py:19
  37.6 1.6 %collective-permute-start.9 = (bf16[16,32,256]{2,1,0:T(8,128)(2,1)S(1)}, bf16[16,32,256]{2,1,0:T(8,128)(2,1)S(1)}, u32[]{:S(2)}, u32[]{:S(2)}) collective-permute-start(bf16[16,32,256]{2,1,0:T(8,128)(2,1)S(1)} %shard_map.75.refs_0_.refs_4_.refs_7_), channel_id=1, source_target_pairs={{0,1},{1,0},{2,3},{3,2},{4,5},{5,4},{6,7},{7,6},{8,9},{9,8},{10,11... | collective-permute-start | bytes 786440 | tf_op jit(solution)/shard_map/ppermute | solution.py:19
  39.1 1.7 %shard_map.78.refs_1_.refs_2_ = f32[2,128,256]{2,1,0:T(8,128)S(1)} custom-call(bf16[2,512,256]{2,1,0:T(8,128)(2,1)S(1)} %get-tuple-element.41.refs_0_, bf16[27,128,512]{2,1,0:T(8,128)(2,1)S(1)} %copy-done), custom_call_target="tpu_custom_call" | custom-call | flops 1207959552 | bytes 3538944 | tf_op jit(solution)/shard_map/pallas_call | solution.py:60
  40.9 3.4 %collective-permute-start.14 = (bf16[1,512,256]{2,1,0:T(8,128)(2,1)S(1)}, bf16[1,512,256]{2,1,0:T(8,128)(2,1)S(1)}, u32[]{:S(2)}, u32[]{:S(2)}) collective-permute-start(bf16[1,512,256]{2,1,0:T(8,128)(2,1)S(1)} %shard_map.79), channel_id=1, source_target_pairs={{0,8},{8,16},{16,24},{12,4},{20,12},{28,20},{1,9},{9,17},{17,25},{... | collective-permute-start | bytes 786440 | tf_op jit(solution)/shard_map/ppermute | solution.py:35
  45.4 2.4 %collective-permute-start.16 = (bf16[2,2,32,256]{3,2,1,0:T(8,128)(2,1)S(1)}, bf16[2,2,32,256]{3,2,1,0:T(8,128)(2,1)S(1)}, u32[]{:S(2)}, u32[]{:S(2)}) collective-permute-start(bf16[2,2,32,256]{3,2,1,0:T(8,128)(2,1)S(1)} %get-tuple-element.43), channel_id=1, source_target_pairs={{0,16},{4,20},{8,24},{12,28},{16,0},{20,4},{24,8},{28,12},{1,17},{... | collective-permute-start | bytes 196616 | tf_op jit(solution)/shard_map/ppermute | solution.py:19
  49.3 1.9 %collective-permute-done.15.refs_4_.refs_3_ = bf16[2,2,32,256]{3,2,1,0:T(8,128)(2,1)S(1)} collective-permute-done((bf16[2,2,32,256]{3,2,1,0:T(8,128)(2,1)S(1)}, bf16[2,2,32,256]{3,2,1,0:T(8,128)(2,1)S(1)}, u32[]{:S(2)}, u32[]{:S(2)}) %collective-permute-start.15) | collective-permute-done | bytes 65568 | tf_op jit(solution)/shard_map/ppermute | solution.py:19
  51.2 3.9 %collective-permute-done.16.refs_5_.refs_2_.refs_3_ = bf16[2,2,32,256]{3,2,1,0:T(8,128)(2,1)S(1)} collective-permute-done((bf16[2,2,32,256]{3,2,1,0:T(8,128)(2,1)S(1)}, bf16[2,2,32,256]{3,2,1,0:T(8,128)(2,1)S(1)}, u32[]{:S(2)}, u32[]{:S(2)}) %collective-permute-start.16) | collective-permute-done | bytes 65568 | tf_op jit(solution)/shard_map/ppermute | solution.py:19
  56.1 1.4 %collective-permute-start.18 = (f32[2,8,256]{2,1,0:T(8,128)S(1)}, f32[2,8,256]{2,1,0:T(8,128)S(1)}, u32[]{:S(2)}, u32[]{:S(2)}) collective-permute-start(f32[2,8,256]{2,1,0:T(8,128)S(1)} %get-tuple-element.46.refs_6_.refs_4_), channel_id=1, source_target_pairs={{0,3},{1,2},{2,1},{3,0},{4,7},{5,6},{6,5},{7,4},{8,11},{9,10},{10,... | collective-permute-start | bytes 49160 | tf_op jit(solution)/shard_map/ppermute | solution.py:19
  58.1 1.5 %collective-permute-start.20 = (f32[2,8,256]{2,1,0:T(8,128)S(1)}, f32[2,8,256]{2,1,0:T(8,128)S(1)}, u32[]{:S(2)}, u32[]{:S(2)}) collective-permute-start(f32[2,8,256]{2,1,0:T(8,128)S(1)} %get-tuple-element.46.refs_6_.refs_4_), channel_id=1, source_target_pairs={{0,1},{1,0},{2,3},{3,2},{4,5},{5,4},{6,7},{7,6},{8,9},{9,8},{10,11... | collective-permute-start | bytes 49160 | tf_op jit(solution)/shard_map/ppermute | solution.py:19
  62.2 1.6 %collective-permute-start.24 = (bf16[16,32,256]{2,1,0:T(8,128)(2,1)S(1)}, bf16[16,32,256]{2,1,0:T(8,128)(2,1)S(1)}, u32[]{:S(2)}, u32[]{:S(2)}) collective-permute-start(bf16[16,32,256]{2,1,0:T(8,128)(2,1)S(1)} %shard_map.87.refs_3_.refs_0_), channel_id=1, source_target_pairs={{0,1},{1,0},{2,3},{3,2},{4,5},{5,4},{6,7},{7,6},{8,9},{9,8},{10,11... | collective-permute-start | bytes 786440 | tf_op jit(solution)/shard_map/ppermute | solution.py:19
  65.0 1.6 %shard_map.83.refs_1_.refs_2_ = f32[2,256,512]{2,1,0:T(8,128)S(1)} custom-call(bf16[2,256,128]{2,1,0:T(8,128)(2,1)S(1)} %shard_map.82.refs_0_.refs_5_.refs_2_, bf16[27,128,512]{2,1,0:T(8,128)(2,1)S(1)} %copy-done), custom_call_target="tpu_custom_call" | custom-call | flops 1207959552 | bytes 3538944 | tf_op jit(solution)/shard_map/pallas_call | solution.py:60
  66.6 4.2 %collective-permute-start.22 = (bf16[1,256,128]{2,1,0:T(8,128)(2,1)S(1)}, bf16[1,256,128]{2,1,0:T(8,128)(2,1)S(1)}, u32[]{:S(2)}, u32[]{:S(2)}) collective-permute-start(bf16[1,256,128]{2,1,0:T(8,128)(2,1)S(1)} %shard_map.84), channel_id=1, source_target_pairs={{0,8},{8,16},{16,24},{12,4},{20,12},{28,20},{1,9},{9,17},{17,25},{... | collective-permute-start | bytes 196616 | tf_op jit(solution)/shard_map/ppermute | solution.py:35
  71.0 2.6 %collective-permute-done.25.refs_5_.refs_8_.refs_1_ = bf16[2,256,128]{2,1,0:T(8,128)(2,1)S(1)} collective-permute-done((bf16[2,256,128]{2,1,0:T(8,128)(2,1)S(1)}, bf16[2,256,128]{2,1,0:T(8,128)(2,1)S(1)}, u32[]{:S(2)}, u32[]{:S(2)}) %collective-permute-start.25) | collective-permute-done | bytes 131104 | tf_op jit(solution)/shard_map/ppermute | solution.py:19
  74.9 1.5 %collective-permute-start.26 = (bf16[2,256,128]{2,1,0:T(8,128)(2,1)S(1)}, bf16[2,256,128]{2,1,0:T(8,128)(2,1)S(1)}, u32[]{:S(2)}, u32[]{:S(2)}) collective-permute-start(bf16[2,256,128]{2,1,0:T(8,128)(2,1)S(1)} %get-tuple-element.48), channel_id=1, source_target_pairs={{0,3},{1,2},{2,1},{3,0},{4,7},{5,6},{6,5},{7,4},{8,11},{9,10},{10,... | collective-permute-start | bytes 393224 | tf_op jit(solution)/shard_map/ppermute | solution.py:19
  76.9 1.5 %collective-permute-start.28 = (bf16[2,256,128]{2,1,0:T(8,128)(2,1)S(1)}, bf16[2,256,128]{2,1,0:T(8,128)(2,1)S(1)}, u32[]{:S(2)}, u32[]{:S(2)}) collective-permute-start(bf16[2,256,128]{2,1,0:T(8,128)(2,1)S(1)} %get-tuple-element.50), channel_id=1, source_target_pairs={{0,1},{1,0},{2,3},{3,2},{4,5},{5,4},{6,7},{7,6},{8,9},{9,8},{10,11... | collective-permute-start | bytes 393224 | tf_op jit(solution)/shard_map/ppermute | solution.py:19
  80.8 1.4 %collective-permute-done.26.refs_1_ = bf16[2,256,128]{2,1,0:T(8,128)(2,1)S(1)} collective-permute-done((bf16[2,256,128]{2,1,0:T(8,128)(2,1)S(1)}, bf16[2,256,128]{2,1,0:T(8,128)(2,1)S(1)}, u32[]{:S(2)}, u32[]{:S(2)}) %collective-permute-start.26) | collective-permute-done | bytes 131104 | tf_op jit(solution)/shard_map/ppermute | solution.py:19
  82.2 1.5 %collective-permute-done.27.refs_2_ = bf16[2,256,128]{2,1,0:T(8,128)(2,1)S(1)} collective-permute-done((bf16[2,256,128]{2,1,0:T(8,128)(2,1)S(1)}, bf16[2,256,128]{2,1,0:T(8,128)(2,1)S(1)}, u32[]{:S(2)}, u32[]{:S(2)}) %collective-permute-start.27) | collective-permute-done | bytes 131104 | tf_op jit(solution)/shard_map/ppermute | solution.py:19
  84.0 2.4 %collective-permute-start.31 = (bf16[2,256,128]{2,1,0:T(8,128)(2,1)S(1)}, bf16[2,256,128]{2,1,0:T(8,128)(2,1)S(1)}, u32[]{:S(2)}, u32[]{:S(2)}) collective-permute-start(bf16[2,256,128]{2,1,0:T(8,128)(2,1)S(1)} %shard_map.90.refs_3_.refs_2_), channel_id=1, source_target_pairs={{0,24},{4,28},{8,16},{12,20},{16,8},{20,12},{24,0},{28,4},{1,25},{... | collective-permute-start | bytes 393224 | tf_op jit(solution)/shard_map/ppermute | solution.py:19
  88.4 4.0 %shard_map.92 = (f32[27,64,128]{2,1,0:T(8,128)}, f32[8,128]{1,0:T(8,128)S(1)}) custom-call(bf16[576,4096]{1,0:T(8,128)(2,1)S(1)} %get-tuple-element.54.refs_0_, bf16[768,256]{1,0:T(8,128)(2,1)S(1)} %collective-permute-done.34.refs_1_, bf16[2,256,128]{2,1,0:T(8,128)(2,1)S(1)} %shard_map.82.refs_0_.refs_5_.refs_2_, ...), custom_call_target="tpu_custom_call" | custom-call | flops 1811939328 | bytes 5603328 | tf_op jit(solution)/shard_map/pallas_call | solution.py:60
  92.4 7.0 %collective-permute-done.32.refs_1_.refs_4_ = bf16[2,256,128]{2,1,0:T(8,128)(2,1)S(1)} collective-permute-done((bf16[2,256,128]{2,1,0:T(8,128)(2,1)S(1)}, bf16[2,256,128]{2,1,0:T(8,128)(2,1)S(1)}, u32[]{:S(2)}, u32[]{:S(2)}) %collective-permute-start.32) | collective-permute-done | bytes 131104 | tf_op jit(solution)/shard_map/ppermute | solution.py:19
  99.5 1.9 %collective-permute-done.35.refs_1_ = bf16[1024,256]{1,0:T(8,128)(2,1)S(1)} collective-permute-done((bf16[1024,256]{1,0:T(8,128)(2,1)S(1)}, bf16[1024,256]{1,0:T(8,128)(2,1)S(1)}, u32[]{:S(2)}, u32[]{:S(2)}) %collective-permute-start.35) | collective-permute-done | bytes 524320 | tf_op jit(solution)/shard_map/ppermute | solution.py:19
  101.4 3.9 %shard_map.94 = (f32[27,64,128]{2,1,0:T(8,128)}, f32[8,128]{1,0:T(8,128)}) custom-call(bf16[576,4096]{1,0:T(8,128)(2,1)S(1)} %get-tuple-element.38.refs_0_, bf16[1024,256]{1,0:T(8,128)(2,1)S(1)} %collective-permute-done.35.refs_1_, bf16[2,256,128]{2,1,0:T(8,128)(2,1)S(1)} %shard_map.90.refs_3_.refs_2_, ...), custom_call_target="tpu_custom_call" | custom-call | flops 1811939328 | bytes 5603328 | tf_op jit(solution)/shard_map/pallas_call | solution.py:60
  (77 shorter events, 25.3 us)
Async XLA Ops:
  0.6 8.8 %collective-permute-start = (bf16[2,128,256]{2,1,0:T(8,128)(2,1)}, bf16[2,128,256]{2,1,0:T(8,128)(2,1)S(1)}, u32[]{:S(2)}, u32[]{:S(2)}) collective-permute-start(bf16[2,128,256]{2,1,0:T(8,128)(2,1)} %refs_0_.2), channel_id=1, source_target_pairs={{0,3},{1,2},{2,1},{3,0},{4,7},{5,6},{6,5},{7,4},{8,11},{9,10},{10,... | collective-permute-start | bytes 393224 | tf_op jit(solution)/shard_map/ppermute | solution.py:19
  4.6 6.5 %collective-permute-start.1 = (bf16[2,128,256]{2,1,0:T(8,128)(2,1)}, bf16[2,128,256]{2,1,0:T(8,128)(2,1)S(1)}, u32[]{:S(2)}, u32[]{:S(2)}) collective-permute-start(bf16[2,128,256]{2,1,0:T(8,128)(2,1)} %refs_0_.2), channel_id=1, source_target_pairs={{0,2},{1,3},{2,0},{3,1},{4,6},{5,7},{6,4},{7,5},{8,10},{9,11},{10,... | collective-permute-start | bytes 393224 | tf_op jit(solution)/shard_map/ppermute | solution.py:19
  5.1 6.3 %collective-permute-start.2 = (bf16[2,128,256]{2,1,0:T(8,128)(2,1)}, bf16[2,128,256]{2,1,0:T(8,128)(2,1)S(1)}, u32[]{:S(2)}, u32[]{:S(2)}) collective-permute-start(bf16[2,128,256]{2,1,0:T(8,128)(2,1)} %refs_0_.2), channel_id=1, source_target_pairs={{0,1},{1,0},{2,3},{3,2},{4,5},{5,4},{6,7},{7,6},{8,9},{9,8},{10,11... | collective-permute-start | bytes 393224 | tf_op jit(solution)/shard_map/ppermute | solution.py:19
  13.4 13.5 %collective-permute-start.7 = (bf16[1,512,256]{2,1,0:T(8,128)(2,1)S(1)}, bf16[1,512,256]{2,1,0:T(8,128)(2,1)S(1)}, u32[]{:S(2)}, u32[]{:S(2)}) collective-permute-start(bf16[1,512,256]{2,1,0:T(8,128)(2,1)S(1)} %shard_map.71), channel_id=1, source_target_pairs={{0,8},{8,16},{16,24},{12,4},{20,12},{28,20},{1,9},{9,17},{17,25},{... | collective-permute-start | bytes 786440 | tf_op jit(solution)/shard_map/ppermute | solution.py:35
  16.9 6.3 %collective-permute-start.3 = (bf16[2,2,32,256]{3,2,1,0:T(8,128)(2,1)S(1)}, bf16[2,2,32,256]{3,2,1,0:T(8,128)(2,1)S(1)}, u32[]{:S(2)}, u32[]{:S(2)}) collective-permute-start(bf16[2,2,32,256]{3,2,1,0:T(8,128)(2,1)S(1)} %get-tuple-element.32), channel_id=1, source_target_pairs={{0,8},{4,12},{8,0},{12,4},{16,24},{20,28},{24,16},{28,20},{1,9},{5... | collective-permute-start | bytes 196616 | tf_op jit(solution)/shard_map/ppermute | solution.py:19
  18.6 5.7 %collective-permute-start.4 = (bf16[2,2,32,256]{3,2,1,0:T(8,128)(2,1)S(1)}, bf16[2,2,32,256]{3,2,1,0:T(8,128)(2,1)S(1)}, u32[]{:S(2)}, u32[]{:S(2)}) collective-permute-start(bf16[2,2,32,256]{3,2,1,0:T(8,128)(2,1)S(1)} %get-tuple-element.33), channel_id=1, source_target_pairs={{0,16},{4,20},{8,24},{12,28},{16,0},{20,4},{24,8},{28,12},{1,17},{... | collective-permute-start | bytes 196616 | tf_op jit(solution)/shard_map/ppermute | solution.py:19
  19.6 7.3 %collective-permute-start.5 = (bf16[2,2,32,256]{3,2,1,0:T(8,128)(2,1)S(1)}, bf16[2,2,32,256]{3,2,1,0:T(8,128)(2,1)S(1)}, u32[]{:S(2)}, u32[]{:S(2)}) collective-permute-start(bf16[2,2,32,256]{3,2,1,0:T(8,128)(2,1)S(1)} %get-tuple-element.34), channel_id=1, source_target_pairs={{0,24},{4,28},{8,16},{12,20},{16,8},{20,12},{24,0},{28,4},{1,25},{... | collective-permute-start | bytes 196616 | tf_op jit(solution)/shard_map/ppermute | solution.py:19
  27.7 3.8 %collective-permute-start.8 = (bf16[8,32,256]{2,1,0:T(8,128)(2,1)S(1)}, bf16[8,32,256]{2,1,0:T(8,128)(2,1)S(1)}, u32[]{:S(2)}, u32[]{:S(2)}) collective-permute-start(bf16[8,32,256]{2,1,0:T(8,128)(2,1)S(1)} %shard_map.74), channel_id=1, source_target_pairs={{0,4},{4,0},{8,12},{12,8},{16,20},{20,16},{24,28},{28,24},{1,5},{5... | collective-permute-start | bytes 393224 | tf_op jit(solution)/shard_map/ppermute | solution.py:19
  28.0 7.2 %collective-permute-start.10 = (bf16[2,128,256]{2,1,0:T(8,128)(2,1)S(1)}, bf16[2,128,256]{2,1,0:T(8,128)(2,1)S(1)}, u32[]{:S(2)}, u32[]{:S(2)}) collective-permute-start(bf16[2,128,256]{2,1,0:T(8,128)(2,1)S(1)} %get-tuple-element.37.refs_4_.refs_3_), channel_id=1, source_target_pairs={{0,3},{1,2},{2,1},{3,0},{4,7},{5,6},{6,5},{7,4},{8,11},{9,10},{10,... | collective-permute-start | bytes 393224 | tf_op jit(solution)/shard_map/ppermute | solution.py:19
  29.7 7.7 %collective-permute-start.11 = (bf16[2,128,256]{2,1,0:T(8,128)(2,1)S(1)}, bf16[2,128,256]{2,1,0:T(8,128)(2,1)S(1)}, u32[]{:S(2)}, u32[]{:S(2)}) collective-permute-start(bf16[2,128,256]{2,1,0:T(8,128)(2,1)S(1)} %get-tuple-element.37.refs_4_.refs_3_), channel_id=1, source_target_pairs={{0,2},{1,3},{2,0},{3,1},{4,6},{5,7},{6,4},{7,5},{8,10},{9,11},{10,... | collective-permute-start | bytes 393224 | tf_op jit(solution)/shard_map/ppermute | solution.py:19
  31.0 6.4 %collective-permute-start.12 = (bf16[2,128,256]{2,1,0:T(8,128)(2,1)S(1)}, bf16[2,128,256]{2,1,0:T(8,128)(2,1)S(1)}, u32[]{:S(2)}, u32[]{:S(2)}) collective-permute-start(bf16[2,128,256]{2,1,0:T(8,128)(2,1)S(1)} %get-tuple-element.37.refs_4_.refs_3_), channel_id=1, source_target_pairs={{0,1},{1,0},{2,3},{3,2},{4,5},{5,4},{6,7},{7,6},{8,9},{9,8},{10,11... | collective-permute-start | bytes 393224 | tf_op jit(solution)/shard_map/ppermute | solution.py:19
  37.6 17.5 %collective-permute-start.9 = (bf16[16,32,256]{2,1,0:T(8,128)(2,1)S(1)}, bf16[16,32,256]{2,1,0:T(8,128)(2,1)S(1)}, u32[]{:S(2)}, u32[]{:S(2)}) collective-permute-start(bf16[16,32,256]{2,1,0:T(8,128)(2,1)S(1)} %shard_map.75.refs_0_.refs_4_.refs_7_), channel_id=1, source_target_pairs={{0,1},{1,0},{2,3},{3,2},{4,5},{5,4},{6,7},{7,6},{8,9},{9,8},{10,11... | collective-permute-start | bytes 786440 | tf_op jit(solution)/shard_map/ppermute | solution.py:19
  40.9 14.2 %collective-permute-start.14 = (bf16[1,512,256]{2,1,0:T(8,128)(2,1)S(1)}, bf16[1,512,256]{2,1,0:T(8,128)(2,1)S(1)}, u32[]{:S(2)}, u32[]{:S(2)}) collective-permute-start(bf16[1,512,256]{2,1,0:T(8,128)(2,1)S(1)} %shard_map.79), channel_id=1, source_target_pairs={{0,8},{8,16},{16,24},{12,4},{20,12},{28,20},{1,9},{9,17},{17,25},{... | collective-permute-start | bytes 786440 | tf_op jit(solution)/shard_map/ppermute | solution.py:35
  44.3 6.9 %collective-permute-start.15 = (bf16[2,2,32,256]{3,2,1,0:T(8,128)(2,1)S(1)}, bf16[2,2,32,256]{3,2,1,0:T(8,128)(2,1)S(1)}, u32[]{:S(2)}, u32[]{:S(2)}) collective-permute-start(bf16[2,2,32,256]{3,2,1,0:T(8,128)(2,1)S(1)} %get-tuple-element.42), channel_id=1, source_target_pairs={{0,24},{4,28},{8,16},{12,20},{16,8},{20,12},{24,0},{28,4},{1,25},{... | collective-permute-start | bytes 196616 | tf_op jit(solution)/shard_map/ppermute | solution.py:19
  45.4 9.7 %collective-permute-start.16 = (bf16[2,2,32,256]{3,2,1,0:T(8,128)(2,1)S(1)}, bf16[2,2,32,256]{3,2,1,0:T(8,128)(2,1)S(1)}, u32[]{:S(2)}, u32[]{:S(2)}) collective-permute-start(bf16[2,2,32,256]{3,2,1,0:T(8,128)(2,1)S(1)} %get-tuple-element.43), channel_id=1, source_target_pairs={{0,16},{4,20},{8,24},{12,28},{16,0},{20,4},{24,8},{28,12},{1,17},{... | collective-permute-start | bytes 196616 | tf_op jit(solution)/shard_map/ppermute | solution.py:19
  47.9 7.2 %collective-permute-start.17 = (bf16[2,2,32,256]{3,2,1,0:T(8,128)(2,1)S(1)}, bf16[2,2,32,256]{3,2,1,0:T(8,128)(2,1)S(1)}, u32[]{:S(2)}, u32[]{:S(2)}) collective-permute-start(bf16[2,2,32,256]{3,2,1,0:T(8,128)(2,1)S(1)} %get-tuple-element.44), channel_id=1, source_target_pairs={{0,8},{4,12},{8,0},{12,4},{16,24},{20,28},{24,16},{28,20},{1,9},{5... | collective-permute-start | bytes 196616 | tf_op jit(solution)/shard_map/ppermute | solution.py:19
  55.9 6.2 %collective-permute-start.23 = (bf16[8,32,256]{2,1,0:T(8,128)(2,1)S(1)}, bf16[8,32,256]{2,1,0:T(8,128)(2,1)S(1)}, u32[]{:S(2)}, u32[]{:S(2)}) collective-permute-start(bf16[8,32,256]{2,1,0:T(8,128)(2,1)S(1)} %shard_map.86), channel_id=1, source_target_pairs={{0,4},{4,0},{8,12},{12,8},{16,20},{20,16},{24,28},{28,24},{1,5},{5... | collective-permute-start | bytes 393224 | tf_op jit(solution)/shard_map/ppermute | solution.py:19
  56.1 4.6 %collective-permute-start.18 = (f32[2,8,256]{2,1,0:T(8,128)S(1)}, f32[2,8,256]{2,1,0:T(8,128)S(1)}, u32[]{:S(2)}, u32[]{:S(2)}) collective-permute-start(f32[2,8,256]{2,1,0:T(8,128)S(1)} %get-tuple-element.46.refs_6_.refs_4_), channel_id=1, source_target_pairs={{0,3},{1,2},{2,1},{3,0},{4,7},{5,6},{6,5},{7,4},{8,11},{9,10},{10,... | collective-permute-start | bytes 49160 | tf_op jit(solution)/shard_map/ppermute | solution.py:19
  57.5 3.7 %collective-permute-start.19 = (f32[2,8,256]{2,1,0:T(8,128)S(1)}, f32[2,8,256]{2,1,0:T(8,128)S(1)}, u32[]{:S(2)}, u32[]{:S(2)}) collective-permute-start(f32[2,8,256]{2,1,0:T(8,128)S(1)} %get-tuple-element.46.refs_6_.refs_4_), channel_id=1, source_target_pairs={{0,2},{1,3},{2,0},{3,1},{4,6},{5,7},{6,4},{7,5},{8,10},{9,11},{10,... | collective-permute-start | bytes 49160 | tf_op jit(solution)/shard_map/ppermute | solution.py:19
  58.1 3.7 %collective-permute-start.20 = (f32[2,8,256]{2,1,0:T(8,128)S(1)}, f32[2,8,256]{2,1,0:T(8,128)S(1)}, u32[]{:S(2)}, u32[]{:S(2)}) collective-permute-start(f32[2,8,256]{2,1,0:T(8,128)S(1)} %get-tuple-element.46.refs_6_.refs_4_), channel_id=1, source_target_pairs={{0,1},{1,0},{2,3},{3,2},{4,5},{5,4},{6,7},{7,6},{8,9},{9,8},{10,11... | collective-permute-start | bytes 49160 | tf_op jit(solution)/shard_map/ppermute | solution.py:19
  62.2 12.0 %collective-permute-start.24 = (bf16[16,32,256]{2,1,0:T(8,128)(2,1)S(1)}, bf16[16,32,256]{2,1,0:T(8,128)(2,1)S(1)}, u32[]{:S(2)}, u32[]{:S(2)}) collective-permute-start(bf16[16,32,256]{2,1,0:T(8,128)(2,1)S(1)} %shard_map.87.refs_3_.refs_0_), channel_id=1, source_target_pairs={{0,1},{1,0},{2,3},{3,2},{4,5},{5,4},{6,7},{7,6},{8,9},{9,8},{10,11... | collective-permute-start | bytes 786440 | tf_op jit(solution)/shard_map/ppermute | solution.py:19
  63.8 9.9 %collective-permute-start.25 = (bf16[2,256,128]{2,1,0:T(8,128)(2,1)S(1)}, bf16[2,256,128]{2,1,0:T(8,128)(2,1)S(1)}, u32[]{:S(2)}, u32[]{:S(2)}) collective-permute-start(bf16[2,256,128]{2,1,0:T(8,128)(2,1)S(1)} %shard_map.82.refs_0_.refs_5_.refs_2_), channel_id=1, source_target_pairs={{0,16},{4,20},{8,24},{12,28},{16,0},{20,4},{24,8},{28,12},{1,17},{... | collective-permute-start | bytes 393224 | tf_op jit(solution)/shard_map/ppermute | solution.py:19
  66.6 7.6 %collective-permute-start.22 = (bf16[1,256,128]{2,1,0:T(8,128)(2,1)S(1)}, bf16[1,256,128]{2,1,0:T(8,128)(2,1)S(1)}, u32[]{:S(2)}, u32[]{:S(2)}) collective-permute-start(bf16[1,256,128]{2,1,0:T(8,128)(2,1)S(1)} %shard_map.84), channel_id=1, source_target_pairs={{0,8},{8,16},{16,24},{12,4},{20,12},{28,20},{1,9},{9,17},{17,25},{... | collective-permute-start | bytes 196616 | tf_op jit(solution)/shard_map/ppermute | solution.py:35
  70.8 10.0 %collective-permute-start.29 = (bf16[2,256,128]{2,1,0:T(8,128)(2,1)S(1)}, bf16[2,256,128]{2,1,0:T(8,128)(2,1)S(1)}, u32[]{:S(2)}, u32[]{:S(2)}) collective-permute-start(bf16[2,256,128]{2,1,0:T(8,128)(2,1)S(1)} %shard_map.82.refs_0_.refs_5_.refs_2_), channel_id=1, source_target_pairs={{0,8},{4,12},{8,0},{12,4},{16,24},{20,28},{24,16},{28,20},{1,9},{5... | collective-permute-start | bytes 393224 | tf_op jit(solution)/shard_map/ppermute | solution.py:19
  73.7 7.2 %collective-permute-start.30 = (bf16[2,256,128]{2,1,0:T(8,128)(2,1)S(1)}, bf16[2,256,128]{2,1,0:T(8,128)(2,1)S(1)}, u32[]{:S(2)}, u32[]{:S(2)}) collective-permute-start(bf16[2,256,128]{2,1,0:T(8,128)(2,1)S(1)} %collective-permute-done.25.refs_5_.refs_8_.refs_1_), channel_id=1, source_target_pairs={{0,8},{4,12},{8,0},{12,4},{16,24},{20,28},{24,16},{28,20},{1,9},{5... | collective-permute-start | bytes 393224 | tf_op jit(solution)/shard_map/ppermute | solution.py:19
  74.9 7.4 %collective-permute-start.26 = (bf16[2,256,128]{2,1,0:T(8,128)(2,1)S(1)}, bf16[2,256,128]{2,1,0:T(8,128)(2,1)S(1)}, u32[]{:S(2)}, u32[]{:S(2)}) collective-permute-start(bf16[2,256,128]{2,1,0:T(8,128)(2,1)S(1)} %get-tuple-element.48), channel_id=1, source_target_pairs={{0,3},{1,2},{2,1},{3,0},{4,7},{5,6},{6,5},{7,4},{8,11},{9,10},{10,... | collective-permute-start | bytes 393224 | tf_op jit(solution)/shard_map/ppermute | solution.py:19
  76.4 7.4 %collective-permute-start.27 = (bf16[2,256,128]{2,1,0:T(8,128)(2,1)S(1)}, bf16[2,256,128]{2,1,0:T(8,128)(2,1)S(1)}, u32[]{:S(2)}, u32[]{:S(2)}) collective-permute-start(bf16[2,256,128]{2,1,0:T(8,128)(2,1)S(1)} %get-tuple-element.49), channel_id=1, source_target_pairs={{0,2},{1,3},{2,0},{3,1},{4,6},{5,7},{6,4},{7,5},{8,10},{9,11},{10,... | collective-permute-start | bytes 393224 | tf_op jit(solution)/shard_map/ppermute | solution.py:19
  76.9 6.8 %collective-permute-start.28 = (bf16[2,256,128]{2,1,0:T(8,128)(2,1)S(1)}, bf16[2,256,128]{2,1,0:T(8,128)(2,1)S(1)}, u32[]{:S(2)}, u32[]{:S(2)}) collective-permute-start(bf16[2,256,128]{2,1,0:T(8,128)(2,1)S(1)} %get-tuple-element.50), channel_id=1, source_target_pairs={{0,1},{1,0},{2,3},{3,2},{4,5},{5,4},{6,7},{7,6},{8,9},{9,8},{10,11... | collective-permute-start | bytes 393224 | tf_op jit(solution)/shard_map/ppermute | solution.py:19
  83.9 4.5 %collective-permute-start.34 = (bf16[768,256]{1,0:T(8,128)(2,1)S(1)}, bf16[768,256]{1,0:T(8,128)(2,1)S(1)}, u32[]{:S(2)}, u32[]{:S(2)}) collective-permute-start(bf16[768,256]{1,0:T(8,128)(2,1)S(1)} %shard_map.91), channel_id=1, source_target_pairs={{0,4},{4,0},{8,12},{12,8},{16,20},{20,16},{24,28},{28,24},{1,5},{5... | collective-permute-start | bytes 1179656 | tf_op jit(solution)/shard_map/ppermute | solution.py:19
  84.0 8.4 %collective-permute-start.31 = (bf16[2,256,128]{2,1,0:T(8,128)(2,1)S(1)}, bf16[2,256,128]{2,1,0:T(8,128)(2,1)S(1)}, u32[]{:S(2)}, u32[]{:S(2)}) collective-permute-start(bf16[2,256,128]{2,1,0:T(8,128)(2,1)S(1)} %shard_map.90.refs_3_.refs_2_), channel_id=1, source_target_pairs={{0,24},{4,28},{8,16},{12,20},{16,8},{20,12},{24,0},{28,4},{1,25},{... | collective-permute-start | bytes 393224 | tf_op jit(solution)/shard_map/ppermute | solution.py:19
  86.3 13.1 %collective-permute-start.32 = (bf16[2,256,128]{2,1,0:T(8,128)(2,1)S(1)}, bf16[2,256,128]{2,1,0:T(8,128)(2,1)S(1)}, u32[]{:S(2)}, u32[]{:S(2)}) collective-permute-start(bf16[2,256,128]{2,1,0:T(8,128)(2,1)S(1)} %shard_map.90.refs_3_.refs_2_), channel_id=1, source_target_pairs={{0,16},{4,20},{8,24},{12,28},{16,0},{20,4},{24,8},{28,12},{1,17},{... | collective-permute-start | bytes 393224 | tf_op jit(solution)/shard_map/ppermute | solution.py:19
  87.1 12.3 %collective-permute-start.33 = (bf16[2,256,128]{2,1,0:T(8,128)(2,1)S(1)}, bf16[2,256,128]{2,1,0:T(8,128)(2,1)S(1)}, u32[]{:S(2)}, u32[]{:S(2)}) collective-permute-start(bf16[2,256,128]{2,1,0:T(8,128)(2,1)S(1)} %shard_map.90.refs_3_.refs_2_), channel_id=1, source_target_pairs={{0,8},{4,12},{8,0},{12,4},{16,24},{20,28},{24,16},{28,20},{1,9},{5... | collective-permute-start | bytes 393224 | tf_op jit(solution)/shard_map/ppermute | solution.py:19
  (9 other events, 43.5 us)
